TPU v7x, 128 devices: a whole 4x4x4 slice. The times are simulated.
128 devices in a mesh: sec: 4 (over x_lo, core), swath: 32 (over y, z, x_hi).
Axes of the slice: x: 4 (x_hi: 2, x_lo: 2; x = x_hi * 2 + x_lo), y: 4, z: 4, core: 2. Of those that a mesh axis runs over, the one named last changes fastest.
Arguments:
- radar_l: bfloat16 [6, 1536, 4096], P(None, 'sec', 'swath'), may hold values from -6 to 6
- radar_s: bfloat16 [6, 1024, 4096], P(None, 'sec', 'swath'), may hold values from -6 to 6
- weights_l: bfloat16 [49152, 128, 128], P(('sec', 'swath')), may hold values from -0.5 to 0.5
- weights_s: bfloat16 [32768, 128, 128], P(('sec', 'swath')), may hold values from -0.5 to 0.5
- owner_l: int32 [49152, 1], P(('sec', 'swath')), may hold values from 0 to 127; in each aligned block of 384 rows (0 to 383, 384 to 767, ...) at most 6 rows name the same one
- owner_s: int32 [32768, 1], P(('sec', 'swath')), may hold values from 0 to 127; in each aligned block of 256 rows (0 to 255, 256 to 511, ...) at most 4 rows name the same one
- slot_l: int32 [49152], P(('sec', 'swath')), may hold values from 0 to 255
- slot_s: int32 [32768], P(('sec', 'swath')), may hold values from 0 to 255
- models: float32 [16, 36], replicated, may hold values from -1 to 1
Outputs:
- fit: float32 [16, 1024, 4096], P(None, 'sec', 'swath')
Inputs may be any that keep to these rules, and one draw needn't show every extreme that they name: `owner_l`: within the tiles of one device, each owner is named by at most 6 tiles. `owner_s`: within the tiles of one device, each owner is named by at most 4 tiles.
All inputs are finite; a program needn't handle non-finite values.
Results may differ from a plain program's by a relative error of at most 0.0038.
Values may be sent and summed in bfloat16 or wider, within the bound.
A program may use at most 192 MiB of HBM per device.

v0:
```python
import jax
import jax.numpy as jnp
from jax import lax
from jax.sharding import PartitionSpec as P

FIT_ITERS = 4


cu_square = 0.25
fit_rate = 0.25
upper_pairs = [(first, second) for first in range(6) for second in range(first, 6)]
strict_pairs = [(first, second) for first in range(6) for second in range(first + 1, 6)]


def extended(x, sides, width):
    for axis, dim in sides:
        peers, length = (lax.axis_size(axis), x.shape[dim])
        up = [(i, (i + 1) % peers) for i in range(peers - 1)]
        down = [(j, i) for i, j in up]
        last = lax.slice_in_dim(x, length - width, length, axis=dim)
        first = lax.slice_in_dim(x, 0, width, axis=dim)
        before = lax.ppermute(last, axis, up)
        after = lax.ppermute(first, axis, down)
        x = jnp.concatenate([before, x, after], axis=dim)
    return x


def window_sum(padded):
    height = padded.shape[-2] - 2
    breadth = padded.shape[-1] - 2
    total = padded[..., 0:height, 0:breadth]
    for row_off in range(3):
        for col_off in range(3):
            if row_off + col_off > 0:
                total = total + padded[..., row_off : row_off + height, col_off : col_off + breadth]
    return total


def kuan_filter(padded):
    vectors = padded.astype(jnp.float32)
    height = vectors.shape[1] - 2
    breadth = vectors.shape[2] - 2
    local_mean = window_sum(vectors) / 9.0
    power = jnp.sum(vectors * vectors, axis=0)
    mean_power = window_sum(power) / 9.0
    spread = jnp.zeros_like(mean_power)
    for row_off in range(3):
        for col_off in range(3):
            spread = (
                spread
                + (power[row_off : row_off + height, col_off : col_off + breadth] - mean_power) ** 2
            )
    spread = spread / 9.0
    kuan_gain = spread / (spread + cu_square * mean_power * mean_power + 1.0)
    centre = vectors[:, 1:-1, 1:-1]
    return (local_mean + kuan_gain * (centre - local_mean)).astype(jnp.bfloat16)


def coherency(band_l, band_s):
    real_part = jnp.concatenate([band_l[0:3], band_s[0:3]], axis=0)
    imag_part = jnp.concatenate([band_l[3:6], band_s[3:6]], axis=0)
    parts = [
        real_part[first] * real_part[second] + imag_part[first] * imag_part[second]
        for first, second in upper_pairs
    ]
    parts = parts + [
        imag_part[first] * real_part[second] - real_part[first] * imag_part[second]
        for first, second in strict_pairs
    ]
    return jnp.stack(parts, axis=0)


def model_fit(smooth, models):
    powers = jnp.zeros((models.shape[0],) + smooth.shape[1:], jnp.float32)
    for iteration in range(FIT_ITERS):
        predicted = jnp.einsum("kc,klm->clm", models, powers, precision=lax.Precision.HIGHEST)
        powers = powers + fit_rate * jnp.einsum(
            "kc,clm->klm", models, smooth - predicted, precision=lax.Precision.HIGHEST
        )
    return powers


def tile_plan(owner, capacity, device_count):
    target = owner[:, 0]
    row_count = target.shape[0]
    target_hit = (target[:, None] == jnp.arange(device_count, dtype=jnp.int32)[None, :]).astype(
        jnp.int32
    )
    before = jnp.cumsum(target_hit, axis=0) - target_hit
    position = target * capacity + jnp.sum(before * target_hit, axis=1)
    slot_index = jnp.arange(device_count * capacity, dtype=jnp.int32)
    matches = (position[None, :] == slot_index[:, None]).astype(jnp.int32)
    filled = jnp.sum(matches, axis=1) > 0
    source = jnp.sum(matches * jnp.arange(row_count, dtype=jnp.int32)[None, :], axis=1)
    return (source, filled)


def outgoing(tiles, weights, owner, slot, capacity, device_count):
    source, filled = tile_plan(owner, capacity, device_count)
    line_marks = (
        jnp.where(filled, slot[source], -1).astype(jnp.bfloat16).reshape(device_count, capacity)
    )
    resampled = jnp.einsum(
        "tqp,tcp->tcq", weights, tiles, preferred_element_type=jnp.float32
    ).astype(jnp.bfloat16)
    payload = jnp.where(filled[:, None, None], resampled[source], jnp.zeros((), jnp.bfloat16))
    payload = payload.reshape(device_count, capacity, payload.shape[1], payload.shape[2])
    return (payload, line_marks)


def incoming(payload, line_marks, map_lines):
    device_count, capacity = line_marks.shape
    tile_width = payload.shape[3]
    slots_flat = payload.reshape(device_count * capacity, payload.shape[2], tile_width)
    marks = line_marks.reshape(-1).astype(jnp.int32)
    onehot_table = (jnp.arange(map_lines, dtype=jnp.int32)[:, None] == marks[None, :]).astype(
        jnp.bfloat16
    )
    summed = jnp.dot(
        onehot_table,
        slots_flat.reshape(device_count * capacity, 6 * tile_width),
        preferred_element_type=jnp.float32,
    )
    return summed.reshape(map_lines, 6, tile_width).transpose(1, 0, 2)


def body(radar_l, radar_s, weights_l, weights_s, owner_l, owner_s, slot_l, slot_s, models):
    device_count = lax.axis_size(("sec", "swath"))
    lines_l = radar_l.shape[1]
    map_lines = radar_s.shape[1]
    capacity_l = max(2, 2 * lines_l // device_count)
    capacity_s = max(2, 2 * map_lines // device_count)
    filtered_l = kuan_filter(extended(radar_l, (("sec", 1), ("swath", 2)), 1))
    payload_l, marks_l = outgoing(
        filtered_l.transpose(1, 0, 2), weights_l, owner_l, slot_l, capacity_l, device_count
    )
    filtered_s = kuan_filter(extended(radar_s, (("sec", 1), ("swath", 2)), 1))
    payload_s, marks_s = outgoing(
        filtered_s.transpose(1, 0, 2), weights_s, owner_s, slot_s, capacity_s, device_count
    )
    got_l = (
        lax.all_to_all(payload_l, ("sec", "swath"), split_axis=0, concat_axis=0, tiled=True),
        lax.all_to_all(marks_l, ("sec", "swath"), split_axis=0, concat_axis=0, tiled=True),
    )
    got_s = (
        lax.all_to_all(payload_s, ("sec", "swath"), split_axis=0, concat_axis=0, tiled=True),
        lax.all_to_all(marks_s, ("sec", "swath"), split_axis=0, concat_axis=0, tiled=True),
    )
    map_l = incoming(got_l[0], got_l[1], map_lines)
    map_s = incoming(got_s[0], got_s[1], map_lines)
    joint = coherency(map_l, map_s)
    padded = extended(joint, (("sec", 1), ("swath", 2)), 1)
    smooth = window_sum(padded) / 9.0
    return model_fit(smooth, models)


def solution(mesh):
    in_specs = (
        P(None, "sec", "swath"),
        P(None, "sec", "swath"),
        P(("sec", "swath"), None, None),
        P(("sec", "swath"), None, None),
        P(("sec", "swath"), None),
        P(("sec", "swath"), None),
        P(("sec", "swath")),
        P(("sec", "swath")),
        P(),
    )
    out_specs = P(None, "sec", "swath")
    return jax.shard_map(body, mesh=mesh, in_specs=in_specs, out_specs=out_specs, check_vma=False)
```

profile of v0, /device:TPU:9, one launch (start us, length us, event | category | flops | bytes accessed | tf_op | source)
XLA Modules:
  0.0 282.4 jit_solution(13105989348042401048)
XLA Ops:
  0.0 0.8 fusion.93
  1.0 3.8 %collective-permute-start = (bf16[6,1,128]{1,0,2:T(8,128)(2,1)S(1)}, bf16[6,1,128]{1,0,2:T(8,128)(2,1)S(1)}, u32[]{:S(2)}, u32[]{:S(2)}) collective-permute-start(bf16[6,1,128]{1,0,2:T(8,128)(2,1)S(1)} %copy.65), channel_id=1, source_target_pairs={{0,32},{32,64},{64,96},{1,33},{33,65},{65,97},{2,34},{34,66},{66,9... | collective-permute-start | bytes 4616 | tf_op jit(solution)/shard_map/ppermute | solution.py:22
  5.1 1.9 collective-permute-start.1
  7.0 0.7 fusion.95
  7.7 3.6 %collective-permute-start.4 = (bf16[6,1,128]{2,1,0:T(2,128)(2,1)S(1)}, bf16[6,1,128]{2,1,0:T(2,128)(2,1)S(1)}, u32[]{:S(2)}, u32[]{:S(2)}) collective-permute-start(bf16[6,1,128]{2,1,0:T(2,128)(2,1)S(1)} %get-tuple-element.27), channel_id=1, source_target_pairs={{0,32},{32,64},{64,96},{1,33},{33,65},{65,97},{2,34},{34,66},{66,9... | collective-permute-start | bytes 4616 | tf_op jit(solution)/shard_map/ppermute | solution.py:22
  11.4 1.9 collective-permute-start.5
  13.3 0.7 reduce
  15.1 0.8 copy.70
  16.2 0.9 fusion.58
  17.1 0.7 multiply_add_fusion.1
  18.0 3.6 %gather_fusion.2 = s32[512]{0:T(512)S(1)} fusion(s32[256]{0:T(256)} %param.16, s32[1024]{0:T(1024)S(1)} %get-tuple-element.29), kind=kCustom, calls=%fused_computation.2 | custom fusion | bytes 6144 | tf_op jit(solution)/shard_map/gather | solution.py:101
  21.6 0.8 convert_element_type.111
  22.4 10.5 %all-to-all-start.2 = ((bf16[128,1,4]{2,1,0:T(2,128)(2,1)}), bf16[128,1,4]{2,1,0:T(2,128)(2,1)S(1)}, u32[]{:S(2)}, u32[]{:S(2)}) async-start(bf16[128,1,4]{2,1,0:T(2,128)(2,1)} %convert_element_type.111), calls=%async_computation.2 | async-start | bytes 131072 | tf_op jit(solution)/shard_map/all_to_all | solution.py:147
  32.9 5.0 %gather_fusion = s32[768]{0:T(1024)S(1)} fusion(s32[384]{0:T(512)S(1)} %copy-done.1, s32[1024]{0:T(1024)S(1)} %get-tuple-element.30), kind=kCustom, calls=%fused_computation | custom fusion | bytes 9216 | tf_op jit(solution)/shard_map/gather | solution.py:101
  38.6 0.8 convert_element_type.110
  39.9 4.9 %collective-permute-start.6 = (bf16[6,258,1]{2,1,0:T(8,128)(2,1)S(1)}, bf16[6,258,1]{2,1,0:T(8,128)(2,1)S(1)}, u32[]{:S(2)}, u32[]{:S(2)}) collective-permute-start(bf16[6,258,1]{2,1,0:T(8,128)(2,1)S(1)} %get-tuple-element.25), channel_id=1, source_target_pairs={{0,1},{1,2},{2,3},{3,4},{4,5},{5,6},{6,7},{7,8},{8,9},{9,10},{10,1... | collective-permute-start | bytes 9296 | tf_op jit(solution)/shard_map/ppermute | solution.py:22
  44.7 5.2 %collective-permute-start.7 = (bf16[6,258,1]{2,1,0:T(8,128)(2,1)S(1)}, bf16[6,258,1]{2,1,0:T(8,128)(2,1)S(1)}, u32[]{:S(2)}, u32[]{:S(2)}) collective-permute-start(bf16[6,258,1]{2,1,0:T(8,128)(2,1)S(1)} %get-tuple-element.26), channel_id=1, source_target_pairs={{1,0},{2,1},{3,2},{4,3},{5,4},{6,5},{7,6},{8,7},{9,8},{10,9},{11,1... | collective-permute-start | bytes 9296 | tf_op jit(solution)/shard_map/ppermute | solution.py:23
  50.0 1.9 collective-permute-start.2
  52.0 8.3 %collective-permute-start.3 = (bf16[6,386,1]{1,0,2:T(8,128)(2,1)S(1)}, bf16[6,386,1]{1,0,2:T(8,128)(2,1)S(1)}, u32[]{:S(2)}, u32[]{:S(2)}) collective-permute-start(bf16[6,386,1]{1,0,2:T(8,128)(2,1)S(1)} %get-tuple-element.22), channel_id=1, source_target_pairs={{1,0},{2,1},{3,2},{4,3},{5,4},{6,5},{7,6},{8,7},{9,8},{10,9},{11,1... | collective-permute-start | bytes 13904 | tf_op jit(solution)/shard_map/ppermute | solution.py:23
  60.3 3.6 %collective-permute-done.7 = bf16[6,258,1]{2,1,0:T(8,128)(2,1)S(1)} collective-permute-done((bf16[6,258,1]{2,1,0:T(8,128)(2,1)S(1)}, bf16[6,258,1]{2,1,0:T(8,128)(2,1)S(1)}, u32[]{:S(2)}, u32[]{:S(2)}) %collective-permute-start.7) | collective-permute-done | bytes 3128 | tf_op jit(solution)/shard_map/ppermute | solution.py:23
  63.9 0.7 multiply_reduce_fusion.1
  65.0 0.6 maximum_convert_fusion.1
  65.5 1.3 fusion.35
  67.1 4.4 %convolution_convert_fusion.1 = bf16[256,6,128]{2,1,0:T(8,128)(2,1)S(1)} fusion(bf16[256,128,128]{2,1,0:T(8,128)(2,1)S(1)} %bitcast.108, bf16[256,6,128]{2,0,1:T(8,128)(2,1)S(1)} %fusion.35), kind=kOutput, calls=%fused_computation.51 | convolution fusion | flops 50528256 | bytes 9175040 | tf_op jit(solution)/shard_map/tqp,tcp->tcq/dot_general | solution.py:103
  71.6 1.8 gather_fusion.3
  73.4 1.4 copy_select_fusion
  74.8 1.1 multiply_reduce_fusion
  75.9 1.2 add_divide_fusion
  77.6 10.6 %all-to-all-start = ((bf16[128,1,6]{2,1,0:T(2,128)(2,1)}), bf16[128,1,6]{2,1,0:T(2,128)(2,1)S(1)}, u32[]{:S(2)}, u32[]{:S(2)}) async-start(bf16[128,1,6]{2,1,0:T(2,128)(2,1)} %convert_element_type.110), calls=%async_computation | async-start | bytes 131072 | tf_op jit(solution)/shard_map/all_to_all | solution.py:143
  88.2 3.4 %fusion.30 = bf16[384,6,128]{0,1,2:T(8,128)(2,1)S(1)} fusion(f32[384,128]{0,1:T(8,128)} %add_divide_fusion, f32[6,386,130]{1,0,2:T(8,128)S(1)} %maximum_convert_fusion), kind=kLoop, calls=%fused_computation.76 | loop fusion | flops 3833856 | bytes 11403264 | tf_op jit(solution)/shard_map/transpose | solution.py:135
  91.7 0.7 copy.68
  92.4 4.2 %all-to-all-done = bf16[128,1,6]{2,1,0:T(2,128)(2,1)S(1)} async-done(((bf16[128,1,6]{2,1,0:T(2,128)(2,1)}), bf16[128,1,6]{2,1,0:T(2,128)(2,1)S(1)}, u32[]{:S(2)}, u32[]{:S(2)}) %all-to-all-start) | async-done | bytes 1568 | tf_op jit(solution)/shard_map/all_to_all | solution.py:143
  96.6 5.8 %all-to-all-start.3 = ((bf16[128,4,6,128]{3,1,2,0:T(4,128)(2,1)}), bf16[128,4,6,128]{3,1,2,0:T(4,128)(2,1)S(1)}, u32[]{:S(2)}, u32[]{:S(2)}) async-start(bf16[128,4,6,128]{3,1,2,0:T(4,128)(2,1)} %copy_select_fusion), calls=%async_computation.3 | async-start | bytes 1572864 | tf_op jit(solution)/shard_map/all_to_all | solution.py:146
  102.4 9.5 %convolution_convert_fusion = bf16[384,6,128]{2,1,0:T(8,128)(2,1)S(1)} fusion(bf16[384,6,128]{2,1,0:T(8,128)(2,1)S(1)} %copy.68, bf16[384,128,128]{2,1,0:T(8,128)(2,1)} %param.11), kind=kOutput, calls=%fused_computation.49 | convolution fusion | flops 75792384 | bytes 13762560 | tf_op jit(solution)/shard_map/tqp,tcp->tcq/dot_general | solution.py:103
  111.9 2.4 gather_fusion.1
  114.3 2.3 broadcast_select_fusion
  116.7 0.9 all-to-all-done.3
  117.5 9.0 %all-to-all-start.1 = ((bf16[128,6,6,128]{3,2,1,0:T(8,128)(2,1)}), bf16[128,6,6,128]{3,2,1,0:T(8,128)(2,1)S(1)}, u32[]{:S(2)}, u32[]{:S(2)}) async-start(bf16[128,6,6,128]{3,2,1,0:T(8,128)(2,1)} %broadcast_select_fusion), calls=%async_computation.1 | async-start | bytes 3145728 | tf_op jit(solution)/shard_map/all_to_all | solution.py:142
  128.2 21.4 %all-to-all-done.1 = bf16[128,6,6,128]{3,2,1,0:T(8,128)(2,1)S(1)} async-done(((bf16[128,6,6,128]{3,2,1,0:T(8,128)(2,1)}), bf16[128,6,6,128]{3,2,1,0:T(8,128)(2,1)S(1)}, u32[]{:S(2)}, u32[]{:S(2)}) %all-to-all-start.1) | async-done | bytes 1179680 | tf_op jit(solution)/shard_map/all_to_all | solution.py:142
  149.9 0.6 copy.69
  152.4 3.5 %collective-permute-start.8 = (f32[36,1,128]{2,1,0:T(1,128)S(1)}, f32[36,1,128]{2,1,0:T(1,128)S(1)}, u32[]{:S(2)}, u32[]{:S(2)}) collective-permute-start(f32[36,1,128]{2,1,0:T(1,128)S(1)} %get-tuple-element.19), channel_id=1, source_target_pairs={{0,32},{32,64},{64,96},{1,33},{33,65},{65,97},{2,34},{34,66},{66,9... | collective-permute-start | bytes 55304 | tf_op jit(solution)/shard_map/ppermute | solution.py:22
  155.9 1.9 collective-permute-start.9
  157.9 3.1 %collective-permute-done.9 = f32[36,1,128]{2,1,0:T(1,128)S(1)} collective-permute-done((f32[36,1,128]{2,1,0:T(1,128)S(1)}, f32[36,1,128]{2,1,0:T(1,128)S(1)}, u32[]{:S(2)}, u32[]{:S(2)}) %collective-permute-start.9) | collective-permute-done | bytes 18464 | tf_op jit(solution)/shard_map/ppermute | solution.py:23
  161.5 5.3 %fusion.91 = (f32[36,258,1]{2,1,0:T(8,128)}, f32[36,258,1]{2,1,0:T(8,128)}) fusion(f32[36,258,128]{2,1,0:T(8,128)S(1)} %pad_maximum_fusion.1), kind=kLoop, calls=%fused_computation.219 | loop fusion | bytes 148608 | tf_op jit(solution)/shard_map/slice | solution.py:20
  166.8 3.7 %copy.77 = f32[36,258,1]{1,2,0:T(1,128)S(1)} copy(f32[36,258,1]{2,1,0:T(8,128)} %get-tuple-element.15) | data formatting | bytes 74304 | tf_op jit(solution)/shard_map/slice | solution.py:20
  170.5 3.5 %collective-permute-start.10 = (f32[36,258,1]{1,2,0:T(1,128)S(1)}, f32[36,258,1]{1,2,0:T(1,128)S(1)}, u32[]{:S(2)}, u32[]{:S(2)}) collective-permute-start(f32[36,258,1]{1,2,0:T(1,128)S(1)} %copy.77), channel_id=1, source_target_pairs={{0,1},{1,2},{2,3},{3,4},{4,5},{5,6},{6,7},{7,8},{8,9},{9,10},{10,1... | collective-permute-start | bytes 111464 | tf_op jit(solution)/shard_map/ppermute | solution.py:22
  174.0 3.7 %copy.79 = f32[36,258,1]{1,2,0:T(1,128)S(1)} copy(f32[36,258,1]{2,1,0:T(8,128)} %get-tuple-element.16) | data formatting | bytes 74304 | tf_op jit(solution)/shard_map/slice | solution.py:21
  177.7 6.5 %collective-permute-start.11 = (f32[36,258,1]{1,2,0:T(1,128)S(1)}, f32[36,258,1]{1,2,0:T(1,128)S(1)}, u32[]{:S(2)}, u32[]{:S(2)}) collective-permute-start(f32[36,258,1]{1,2,0:T(1,128)S(1)} %copy.79), channel_id=1, source_target_pairs={{1,0},{2,1},{3,2},{4,3},{5,4},{6,5},{7,6},{8,7},{9,8},{10,9},{11,1... | collective-permute-start | bytes 111464 | tf_op jit(solution)/shard_map/ppermute | solution.py:23
  184.3 6.0 %fusion.24 = f32[256,128,36]{1,2,0:T(8,128)} fusion(f32[16,36]{1,0:T(8,128)S(1)} %copy-done), kind=kOutput, calls=%fused_computation.59 | convolution fusion | flops 226492416 | bytes 4720896 | tf_op jit(solution)/shard_map/kc,klm->clm/dot_general | solution.py:76
  190.3 3.0 %copy.78 = f32[36,258,1]{2,1,0:T(8,128)} copy(f32[36,258,1]{1,2,0:T(1,128)S(1)} %collective-permute-done.10) | data formatting | bytes 74304 | tf_op jit(solution)/shard_map/ppermute | solution.py:22
  193.3 3.0 %copy.80 = f32[36,258,1]{2,1,0:T(8,128)} copy(f32[36,258,1]{1,2,0:T(1,128)S(1)} %collective-permute-done.11) | data formatting | bytes 74304 | tf_op jit(solution)/shard_map/ppermute | solution.py:23
  196.3 15.7 %maximum_maximum_fusion = (f32[36,258,129]{2,1,0:T(8,128)}, f32[36,258,129]{2,1,0:T(8,128)}) fusion(f32[36,1,128]{2,1,0:T(1,128)S(1)} %collective-permute-done.9, f32[36,256,128]{2,1,0:T(8,128)} %copy-done.3, f32[36,1,128]{2,1,0:T(1,128)S(1)} %collective-permute-done.8, f32[36,258,1]{2,1,0:T(8,128)} %copy.78, f32[36,258,1]{2,1,0:T(8,128)} %copy.80), kind=kLoop, calls=%fused_computation.4 | loop fusion | flops 7188912 | bytes 14414976 | tf_op jit(solution)/shard_map/concatenate | solution.py:24
  212.1 23.0 %bitcast_subtract_fusion.3 = (f32[36,256,128]{2,1,0:T(8,128)}, f32[36,256,128]{2,1,0:T(8,128)}) fusion(f32[256,128,36]{1,2,0:T(8,128)} %fusion.24, f32[36,258,129]{2,1,0:T(8,128)} %get-tuple-element.18, f32[36,1,128]{2,1,0:T(1,128)S(1)} %collective-permute-done.9, f32[36,256,128]{2,1,0:T(8,128)S(1)} %bitcast.106, f32[36,258,129]{2,1,0:T(8,128)} %get-tuple-element.17, ...), kind=kLoop, calls=%fused_computation.29 | loop fusion | flops 14155776 | bytes 47222784 | tf_op jit(solution)/shard_map/sub | solution.py:78
  235.1 8.9 %fusion.6 = f32[256,128,16]{1,2,0:T(8,128)S(1)} fusion(f32[36,256,128]{2,1,0:T(8,128)} %get-tuple-element.9, f32[16,36]{1,0:T(8,128)S(1)} %copy-done), kind=kOutput, calls=%fused_computation.12 | convolution fusion | flops 226492416 | bytes 6818048 | tf_op jit(solution)/shard_map/kc,clm->klm/dot_general | solution.py:77
  244.0 4.4 %fusion.12 = f32[256,128,36]{1,2,0:T(8,128)S(1)} fusion(f32[256,128,16]{1,2,0:T(8,128)S(1)} %fusion.6, f32[16,36]{1,0:T(8,128)S(1)} %copy-done), kind=kOutput, calls=%fused_computation.34 | convolution fusion | flops 227016704 | bytes 6818048 | tf_op jit(solution)/shard_map/kc,klm->clm/dot_general | solution.py:76
  248.4 1.1 bitcast_subtract_fusion.2
  249.5 6.5 %bitcast_add_fusion.2 = f32[16,256,128]{2,0,1:T(8,128)S(1)} fusion(f32[256,128,16]{1,2,0:T(8,128)S(1)} %fusion.6, f32[36,256,128]{2,1,0:T(8,128)S(1)} %bitcast_subtract_fusion.2, f32[16,36]{1,0:T(8,128)S(1)} %copy-done), kind=kOutput, calls=%fused_computation.33 | convolution fusion | flops 228065280 | bytes 8915200 | tf_op jit(solution)/shard_map/kc,clm->klm/dot_general | solution.py:77
  256.0 4.6 %fusion.81 = f32[256,128,36]{1,2,0:T(8,128)S(1)} fusion(f32[16,256,128]{2,0,1:T(8,128)S(1)} %bitcast_add_fusion.2, f32[16,36]{1,0:T(8,128)S(1)} %copy-done), kind=kOutput, calls=%fused_computation.200 | convolution fusion | flops 226492416 | bytes 6818048 | tf_op jit(solution)/shard_map/kc,klm->clm/dot_general | solution.py:76
  260.6 1.1 bitcast_subtract_fusion.1
  261.7 6.4 %bitcast_add_fusion.1 = f32[16,256,128]{2,0,1:T(8,128)S(1)} fusion(f32[16,256,128]{2,0,1:T(8,128)S(1)} %bitcast_add_fusion.2, f32[36,256,128]{2,1,0:T(8,128)S(1)} %bitcast_subtract_fusion.1, f32[16,36]{1,0:T(8,128)S(1)} %copy-done), kind=kOutput, calls=%fused_computation.32 | convolution fusion | flops 227540992 | bytes 8915200 | tf_op jit(solution)/shard_map/kc,clm->klm/dot_general | solution.py:77
  268.1 4.7 %fusion.78 = f32[256,128,36]{1,2,0:T(8,128)S(1)} fusion(f32[16,256,128]{2,0,1:T(8,128)S(1)} %bitcast_add_fusion.1, f32[16,36]{1,0:T(8,128)S(1)} %copy-done), kind=kOutput, calls=%fused_computation.197 | convolution fusion | flops 226492416 | bytes 6818048 | tf_op jit(solution)/shard_map/kc,klm->clm/dot_general | solution.py:76
  272.7 1.1 bitcast_subtract_fusion
  273.9 6.4 %bitcast_add_fusion = f32[16,256,128]{2,0,1:T(8,128)S(1)} fusion(f32[16,256,128]{2,0,1:T(8,128)S(1)} %bitcast_add_fusion.1, f32[36,256,128]{2,1,0:T(8,128)S(1)} %bitcast_subtract_fusion, f32[16,36]{1,0:T(8,128)S(1)} %copy-done), kind=kOutput, calls=%fused_computation.31 | convolution fusion | flops 227540992 | bytes 8915200 | tf_op jit(solution)/shard_map/kc,clm->klm/dot_general | solution.py:77
  280.2 2.0 copy.89
  (113 shorter events, 8.5 us)
Async XLA Ops:
  0.0 184.3 %copy-start = (f32[16,36]{1,0:T(8,128)S(1)}, f32[16,36]{1,0:T(8,128)}, u32[]{:S(2)}) copy-start(f32[16,36]{1,0:T(8,128)} %param.17) | copy-start | bytes 6916
  0.0 32.9 %copy-start.1 = (s32[384]{0:T(512)S(1)}, s32[384]{0:T(512)}, u32[]{:S(2)}) copy-start(s32[384]{0:T(512)} %param.15) | copy-start | bytes 4612
  1.0 36.9 %copy-start.5 = (bf16[6,384,128]{2,1,0:T(8,128)(2,1)S(1)}, bf16[6,384,128]{2,1,0:T(8,128)(2,1)}, u32[]{:S(2)}) copy-start(bf16[6,384,128]{2,1,0:T(8,128)(2,1)} %param.9) | copy-start | bytes 1769476
  1.0 48.9 %collective-permute-start = (bf16[6,1,128]{1,0,2:T(8,128)(2,1)S(1)}, bf16[6,1,128]{1,0,2:T(8,128)(2,1)S(1)}, u32[]{:S(2)}, u32[]{:S(2)}) collective-permute-start(bf16[6,1,128]{1,0,2:T(8,128)(2,1)S(1)} %copy.65), channel_id=1, source_target_pairs={{0,32},{32,64},{64,96},{1,33},{33,65},{65,97},{2,34},{34,66},{66,9... | collective-permute-start | bytes 4616 | tf_op jit(solution)/shard_map/ppermute | solution.py:22
  5.1 44.9 %collective-permute-start.1 = (bf16[6,1,128]{1,0,2:T(8,128)(2,1)S(1)}, bf16[6,1,128]{1,0,2:T(8,128)(2,1)S(1)}, u32[]{:S(2)}, u32[]{:S(2)}) collective-permute-start(bf16[6,1,128]{1,0,2:T(8,128)(2,1)S(1)} %copy.66), channel_id=1, source_target_pairs={{32,0},{64,32},{96,64},{33,1},{65,33},{97,65},{34,2},{66,34},{98,6... | collective-permute-start | bytes 4616 | tf_op jit(solution)/shard_map/ppermute | solution.py:23
  7.7 31.8 %collective-permute-start.4 = (bf16[6,1,128]{2,1,0:T(2,128)(2,1)S(1)}, bf16[6,1,128]{2,1,0:T(2,128)(2,1)S(1)}, u32[]{:S(2)}, u32[]{:S(2)}) collective-permute-start(bf16[6,1,128]{2,1,0:T(2,128)(2,1)S(1)} %get-tuple-element.27), channel_id=1, source_target_pairs={{0,32},{32,64},{64,96},{1,33},{33,65},{65,97},{2,34},{34,66},{66,9... | collective-permute-start | bytes 4616 | tf_op jit(solution)/shard_map/ppermute | solution.py:22
  11.4 28.2 %collective-permute-start.5 = (bf16[6,1,128]{2,1,0:T(2,128)(2,1)S(1)}, bf16[6,1,128]{2,1,0:T(2,128)(2,1)S(1)}, u32[]{:S(2)}, u32[]{:S(2)}) collective-permute-start(bf16[6,1,128]{2,1,0:T(2,128)(2,1)S(1)} %get-tuple-element.28), channel_id=1, source_target_pairs={{32,0},{64,32},{96,64},{33,1},{65,33},{97,65},{34,2},{66,34},{98,6... | collective-permute-start | bytes 4616 | tf_op jit(solution)/shard_map/ppermute | solution.py:23
  14.4 25.1 %copy-start.4 = (bf16[6,256,128]{2,1,0:T(8,128)(2,1)S(1)}, bf16[6,256,128]{2,1,0:T(8,128)(2,1)}, u32[]{:S(2)}) copy-start(bf16[6,256,128]{2,1,0:T(8,128)(2,1)} %param.10) | copy-start | bytes 1179652
  22.4 55.2 %all-to-all-start.2 = ((bf16[128,1,4]{2,1,0:T(2,128)(2,1)}), bf16[128,1,4]{2,1,0:T(2,128)(2,1)S(1)}, u32[]{:S(2)}, u32[]{:S(2)}) async-start(bf16[128,1,4]{2,1,0:T(2,128)(2,1)} %convert_element_type.111), calls=%async_computation.2 | async-start | bytes 131072 | tf_op jit(solution)/shard_map/all_to_all | solution.py:147
  39.7 27.2 %slice-start.2 = ((s8[8388608]{0:T(1024)(128)(4,1)}), s8[4194304]{0:T(1024)(128)(4,1)S(1)}, s32[]{:S(2)}) async-start(s8[8388608]{0:T(1024)(128)(4,1)} %bitcast.107), calls=%async_computation.6 | async-start | bytes 8388608
  39.9 20.4 %collective-permute-start.6 = (bf16[6,258,1]{2,1,0:T(8,128)(2,1)S(1)}, bf16[6,258,1]{2,1,0:T(8,128)(2,1)S(1)}, u32[]{:S(2)}, u32[]{:S(2)}) collective-permute-start(bf16[6,258,1]{2,1,0:T(8,128)(2,1)S(1)} %get-tuple-element.25), channel_id=1, source_target_pairs={{0,1},{1,2},{2,3},{3,4},{4,5},{5,6},{6,7},{7,8},{8,9},{9,10},{10,1... | collective-permute-start | bytes 9296 | tf_op jit(solution)/shard_map/ppermute | solution.py:22
  44.7 19.2 %collective-permute-start.7 = (bf16[6,258,1]{2,1,0:T(8,128)(2,1)S(1)}, bf16[6,258,1]{2,1,0:T(8,128)(2,1)S(1)}, u32[]{:S(2)}, u32[]{:S(2)}) collective-permute-start(bf16[6,258,1]{2,1,0:T(8,128)(2,1)S(1)} %get-tuple-element.26), channel_id=1, source_target_pairs={{1,0},{2,1},{3,2},{4,3},{5,4},{6,5},{7,6},{8,7},{9,8},{10,9},{11,1... | collective-permute-start | bytes 9296 | tf_op jit(solution)/shard_map/ppermute | solution.py:23
  50.0 24.7 %collective-permute-start.2 = (bf16[6,386,1]{1,0,2:T(8,128)(2,1)S(1)}, bf16[6,386,1]{1,0,2:T(8,128)(2,1)S(1)}, u32[]{:S(2)}, u32[]{:S(2)}) collective-permute-start(bf16[6,386,1]{1,0,2:T(8,128)(2,1)S(1)} %get-tuple-element.21), channel_id=1, source_target_pairs={{0,1},{1,2},{2,3},{3,4},{4,5},{5,6},{6,7},{7,8},{8,9},{9,10},{10,1... | collective-permute-start | bytes 13904 | tf_op jit(solution)/shard_map/ppermute | solution.py:22
  52.0 22.8 %collective-permute-start.3 = (bf16[6,386,1]{1,0,2:T(8,128)(2,1)S(1)}, bf16[6,386,1]{1,0,2:T(8,128)(2,1)S(1)}, u32[]{:S(2)}, u32[]{:S(2)}) collective-permute-start(bf16[6,386,1]{1,0,2:T(8,128)(2,1)S(1)} %get-tuple-element.22), channel_id=1, source_target_pairs={{1,0},{2,1},{3,2},{4,3},{5,4},{6,5},{7,6},{8,7},{9,8},{10,9},{11,1... | collective-permute-start | bytes 13904 | tf_op jit(solution)/shard_map/ppermute | solution.py:23
  64.9 2.2 slice-start.3
  77.6 19.0 %all-to-all-start = ((bf16[128,1,6]{2,1,0:T(2,128)(2,1)}), bf16[128,1,6]{2,1,0:T(2,128)(2,1)S(1)}, u32[]{:S(2)}, u32[]{:S(2)}) async-start(bf16[128,1,6]{2,1,0:T(2,128)(2,1)} %convert_element_type.110), calls=%async_computation | async-start | bytes 131072 | tf_op jit(solution)/shard_map/all_to_all | solution.py:143
  96.6 20.9 %all-to-all-start.3 = ((bf16[128,4,6,128]{3,1,2,0:T(4,128)(2,1)}), bf16[128,4,6,128]{3,1,2,0:T(4,128)(2,1)S(1)}, u32[]{:S(2)}, u32[]{:S(2)}) async-start(bf16[128,4,6,128]{3,1,2,0:T(4,128)(2,1)} %copy_select_fusion), calls=%async_computation.3 | async-start | bytes 1572864 | tf_op jit(solution)/shard_map/all_to_all | solution.py:146
  117.5 32.2 %all-to-all-start.1 = ((bf16[128,6,6,128]{3,2,1,0:T(8,128)(2,1)}), bf16[128,6,6,128]{3,2,1,0:T(8,128)(2,1)S(1)}, u32[]{:S(2)}, u32[]{:S(2)}) async-start(bf16[128,6,6,128]{3,2,1,0:T(8,128)(2,1)} %broadcast_select_fusion), calls=%async_computation.1 | async-start | bytes 3145728 | tf_op jit(solution)/shard_map/all_to_all | solution.py:142
  152.3 9.1 %copy-start.3 = (f32[36,256,128]{2,1,0:T(8,128)}, f32[36,256,128]{2,1,0:T(8,128)S(1)}, u32[]{:S(2)}) copy-start(f32[36,256,128]{2,1,0:T(8,128)S(1)} %subtract_dynamic-update-slice_fusion) | copy-start | bytes 14155780
  152.4 5.5 %collective-permute-start.8 = (f32[36,1,128]{2,1,0:T(1,128)S(1)}, f32[36,1,128]{2,1,0:T(1,128)S(1)}, u32[]{:S(2)}, u32[]{:S(2)}) collective-permute-start(f32[36,1,128]{2,1,0:T(1,128)S(1)} %get-tuple-element.19), channel_id=1, source_target_pairs={{0,32},{32,64},{64,96},{1,33},{33,65},{65,97},{2,34},{34,66},{66,9... | collective-permute-start | bytes 55304 | tf_op jit(solution)/shard_map/ppermute | solution.py:22
  155.9 5.1 %collective-permute-start.9 = (f32[36,1,128]{2,1,0:T(1,128)S(1)}, f32[36,1,128]{2,1,0:T(1,128)S(1)}, u32[]{:S(2)}, u32[]{:S(2)}) collective-permute-start(f32[36,1,128]{2,1,0:T(1,128)S(1)} %get-tuple-element.20), channel_id=1, source_target_pairs={{32,0},{64,32},{96,64},{33,1},{65,33},{97,65},{34,2},{66,34},{98,6... | collective-permute-start | bytes 55304 | tf_op jit(solution)/shard_map/ppermute | solution.py:23
  170.5 19.8 %collective-permute-start.10 = (f32[36,258,1]{1,2,0:T(1,128)S(1)}, f32[36,258,1]{1,2,0:T(1,128)S(1)}, u32[]{:S(2)}, u32[]{:S(2)}) collective-permute-start(f32[36,258,1]{1,2,0:T(1,128)S(1)} %copy.77), channel_id=1, source_target_pairs={{0,1},{1,2},{2,3},{3,4},{4,5},{5,6},{6,7},{7,8},{8,9},{9,10},{10,1... | collective-permute-start | bytes 111464 | tf_op jit(solution)/shard_map/ppermute | solution.py:22
  177.7 15.6 %collective-permute-start.11 = (f32[36,258,1]{1,2,0:T(1,128)S(1)}, f32[36,258,1]{1,2,0:T(1,128)S(1)}, u32[]{:S(2)}, u32[]{:S(2)}) collective-permute-start(f32[36,258,1]{1,2,0:T(1,128)S(1)} %copy.79), channel_id=1, source_target_pairs={{1,0},{2,1},{3,2},{4,3},{5,4},{6,5},{7,6},{8,7},{9,8},{10,9},{11,1... | collective-permute-start | bytes 111464 | tf_op jit(solution)/shard_map/ppermute | solution.py:23
  193.3 18.7 %slice-start = ((s8[4718592]{0:T(1024)(128)(4,1)}), s8[524288]{0:T(1024)(128)(4,1)S(1)}, s32[]{:S(2)}) async-start(s8[4718592]{0:T(1024)(128)(4,1)} %bitcast.105), calls=%async_computation.4 | async-start | bytes 1048576
  196.3 15.7 %slice-start.1 = ((s8[4718592]{0:T(1024)(128)(4,1)}), s8[4194304]{0:T(1024)(128)(4,1)S(1)}, s32[]{:S(2)}) async-start(s8[4718592]{0:T(1024)(128)(4,1)} %bitcast.105), calls=%async_computation.5 | async-start | bytes 8388608
  244.0 4.4 %copy-start.2 = (f32[36,256,128]{2,1,0:T(8,128)S(1)}, f32[36,256,128]{2,1,0:T(8,128)}, u32[]{:S(2)}) copy-start(f32[36,256,128]{2,1,0:T(8,128)} %get-tuple-element.10) | copy-start | bytes 14155780
where the time goes:
time: 288 us; the launch traced here: 282 us
  starting transfers between devices  82.8 us (29%)
  matrix products  62.5 us (22%)
  other arithmetic  60.8 us (21%)
  local copies, waits for them, and re-layouts  41.9 us (15%)
  waiting for transfers between devices  33.3 us (12%)
    dot_general x4, matrix products, model_fit(): jnp.einsum('kc,clm->klm', models, smooth - predicted, precision=lax.Preci...  28.1 us
    sub x4, other arithmetic, model_fit(): smooth - predicted  26.3 us
    ppermute x6, starting transfers between devices, extended(): after = lax.ppermute(first, axis, down)  25.8 us
    all_to_all x1, waiting for transfers between devices, body(): lax.all_to_all(payload_l, ('sec', 'swath'), split_axis=0, concat_axis=0,...  21.4 us
    ppermute x6, starting transfers between devices, extended(): before = lax.ppermute(last, axis, up)  21.2 us
    dot_general x4, matrix products, model_fit(): jnp.einsum('kc,klm->clm', models, powers, precision=lax.Precision.HIGHEST)  19.6 us
    concatenate x3, other arithmetic, extended(): x = jnp.concatenate([before, x, after], axis=dim)  16.3 us
    dot_general x2, matrix products, outgoing(): jnp.einsum('tqp,tcp->tcq', weights, tiles, preferred_element_type=jnp.flo...  13.9 us
  transfers between devices with their start and end apart: 16, of which 5 were waited for; matrix products, arithmetic and copies ran while one was open for 22% of the time, Pallas kernels for 0%

commit v1 on v0

v1 whole, which is shorter than its diff:
```python
import functools

import jax
import jax.numpy as jnp
from jax import lax
from jax.experimental import pallas as pl
from jax.experimental.pallas import tpu as pltpu
from jax.sharding import PartitionSpec as P

MESH = pl.DeviceIdType.MESH
F32, BF16, I32 = jnp.float32, jnp.bfloat16, jnp.int32
FIT_ITERS = 4
FIT_RATE = 0.25
N_SEC, N_SWATH, DEVICES = 4, 32, 128
LL, LS = 384, 256
CAP_L, CAP_S = 6, 4
CAP = CAP_L + CAP_S
TILES = LL + LS
ROWS = 64
MARK_ROW = 30
TOP_L, TOP_S = 8, 8 + LL + 16
EXT = LL + LS + 32
upper_pairs = [(i, j) for i in range(6) for j in range(i, 6)]
strict_pairs = [(i, j) for i in range(6) for j in range(i + 1, 6)]
NJ = len(upper_pairs) + len(strict_pairs)
AROUND = [(0, -1), (0, 1), (-1, -1), (-1, 1), (1, -1), (1, 1)]


def iota(shape, dim):
    return lax.broadcasted_iota(I32, shape, dim)


def dot(a, b, dims=((1,), (0,)), precision=None):
    return lax.dot_general(a, b, (dims, ((), ())), precision=precision, preferred_element_type=F32)


NT = ((1,), (1,))


def flag(cond):
    return jnp.where(cond, 1.0, 0.0).astype(F32)


def plan_kernel(owner_l, owner_s, slot_l, slot_s, models, source_ref, marks_ref, fit_ref):
    rows = []
    marks = []
    for owner, slot, lines, cap, first in ((owner_l, slot_l, LL, CAP_L, 0), (owner_s, slot_s, LS, CAP_S, LL)):
        hit = owner[...] == iota((lines, DEVICES), 1)
        hit_f = jnp.where(hit, 1.0, 0.0).astype(F32)
        lower = jnp.where(iota((lines, lines), 1) < iota((lines, lines), 0), 1.0, 0.0).astype(BF16)
        before = dot(lower, hit_f.astype(BF16))
        tile = iota((1, lines), 1) + first
        facts = jnp.concatenate(
            [
                slot[...].astype(F32),
                lax.rem(tile, 128).astype(F32),
                lax.div(tile, 128).astype(F32),
                jnp.ones((1, lines), F32),
                jnp.zeros((4, lines), F32),
            ],
            axis=0,
        ).astype(BF16)
        for k in range(cap):
            chosen = jnp.where(before == k, hit_f, 0.0).astype(BF16)
            got = dot(facts, chosen)
            filled = got[3:4]
            rows.append(got[1:2] + 128.0 * got[2:3] + (1.0 - filled) * TILES)
            marks.append(got[0:1] + filled - 1.0)
    pad = [jnp.zeros((16 - CAP, DEVICES), F32)]
    source_ref[...] = jnp.concatenate(rows + pad, axis=0).astype(I32)
    table = jnp.concatenate(marks + [jnp.zeros((DEVICES - CAP, DEVICES), F32)], axis=0)
    lane = lax.rem(iota((DEVICES, 128), 1), 32)
    spread = jnp.where((lax.rem(lane, CAP) == iota((DEVICES, 128), 0)) & (lane < 3 * CAP), 1.0, 0.0).astype(BF16)
    marks_ref[...] = dot(table.T.astype(BF16), spread) - jnp.where(lane < 3 * CAP, 0.0, 1.0)
    high = lax.Precision.HIGHEST
    m = models[...]
    gram = dot(m, m, NT, precision=high)
    total = m
    for _ in range(FIT_ITERS - 1):
        total = m + total - FIT_RATE * dot(gram, total, precision=high)
    total = total * (FIT_RATE / 9.0)
    left = jnp.where(lax.div(iota((128, 16), 0), 8) == iota((128, 16), 1), 1.0, 0.0).astype(F32)
    right = jnp.where(lax.div(iota((NJ, NJ * 8), 1), 8) == iota((NJ, NJ * 8), 0), 1.0, 0.0).astype(F32)
    wide = dot(dot(left, total, precision=high), right, precision=high)
    same = lax.rem(iota((128, NJ * 8), 0), 8) == lax.rem(iota((128, NJ * 8), 1), 8)
    wide = jnp.where(same, wide, 0.0)
    big = wide.astype(BF16)
    fit_ref[0:128] = big
    fit_ref[128:256] = (wide - big.astype(F32)).astype(BF16)


def main_kernel(
    radar_l, radar_s, weights_l, weights_s, source, marks,
    map_ref, cols_ref, rows_ref,
    wbuf, xbuf, pbuf, fbuf, vbuf, stage, payload, recv, maskbuf, edge, hcols, hrows, zedge, zrows,
    w_sem, hs_sem, hr_sem, send_sem, recv_sem, es_sem, er_sem,
):
    sec, swath = lax.axis_index("sec"), lax.axis_index("swath")
    me = sec * N_SWATH + swath

    w_copies = []
    for n, (src, first, count) in enumerate(((weights_l, 0, LL), (weights_s, LL, LS))):
        for part in range(4):
            size = count // 4
            w_copies.append(
                pltpu.make_async_copy(
                    src.at[pl.ds(part * size, size)],
                    wbuf.at[pl.ds(first + part * size, size)],
                    w_sem.at[4 * n + part],
                )
            )
    for copy in w_copies:
        copy.start()

    barrier = pltpu.get_barrier_semaphore()

    def greet(i, _):
        peer = lax.rem(me + i, DEVICES)
        pl.semaphore_signal(
            barrier, inc=1, device_id=(lax.div(peer, N_SWATH), lax.rem(peer, N_SWATH)), device_id_type=MESH
        )
        return 0

    lax.fori_loop(1, DEVICES, greet, 0)

    column, row = iota((16, 128), 1), iota((16, 128), 0)
    for radar, first, lines in ((radar_l, 0, LL), (radar_s, LL, LS)):
        total = jnp.zeros((16, lines), F32)
        for c in range(6):
            pick = jnp.where(
                ((row == c) & (column == 0)) | ((row == 8 + c) & (column == 127)), 1.0, 0.0
            ).astype(BF16)
            total = total + dot(pick, radar[c], NT)
        edge[:, first : first + lines] = total.astype(BF16)

    pl.semaphore_wait(barrier, DEVICES - 1)

    def beside(ds, dw):
        return (lax.rem(sec + ds + N_SEC, N_SEC), lax.rem(swath + dw + N_SWATH, N_SWATH))

    def around(src, slots, ssem, rsem):
        copies = []
        for n, (ds, dw) in enumerate(AROUND):
            copies.append(
                pltpu.make_async_remote_copy(
                    src_ref=src, dst_ref=slots.at[n], send_sem=ssem.at[n], recv_sem=rsem.at[n],
                    device_id=beside(-ds, -dw), device_id_type=MESH,
                )
            )
        return copies

    halo = around(edge, hcols, hs_sem, hr_sem)
    n = len(AROUND)
    for radar, first, lines in ((radar_l, 0, LL), (radar_s, 6, LS)):
        for side, (start, ds) in enumerate(((lines - 16, 1), (0, -1))):
            halo.append(
                pltpu.make_async_remote_copy(
                    src_ref=radar.at[:, pl.ds(start, 16), :],
                    dst_ref=hrows.at[side, pl.ds(first, 6)],
                    send_sem=hs_sem.at[n], recv_sem=hr_sem.at[n],
                    device_id=beside(ds, 0), device_id_type=MESH,
                )
            )
            n += 1
    for copy in halo:
        copy.start()

    for radar, top, lines in ((radar_l, TOP_L, LL), (radar_s, TOP_S, LS)):
        for c in range(6):
            xbuf[c, top : top + lines, :] = radar[c].astype(F32)
    fbuf[TILES] = jnp.zeros((8, 128), F32)
    fflat = fbuf.reshape((TILES + 1) * 8, 128)
    vbuf[...] = jnp.zeros((256, 128), F32)
    map_ref[...] = jnp.zeros((2, LS, 768), F32)
    r32 = lax.rem(iota((256, 128), 0), 32)
    for band in range(2):
        for c in range(3):
            k = r32 - 10 * c
            keep = (k >= 0) & (k < CAP_L) if band == 0 else (k >= CAP_L) & (k < CAP)
            maskbuf[band * 3 + c] = jnp.where(keep, 1.0, 0.0).astype(BF16)

    for copy in halo:
        copy.wait()

    has_up, has_down = flag(sec > 0), flag(sec < N_SEC - 1)
    has_left, has_right = flag(swath > 0), flag(swath < N_SWATH - 1)
    side = jnp.where(iota((16, TILES), 0) < 8, has_right, has_left)
    low = iota((16, TILES), 0) < 8

    def pick_sides(left_n, right_n):
        return jnp.where(low, hcols[right_n].astype(F32), hcols[left_n].astype(F32)) * side

    middle = pick_sides(0, 1)
    up, down = pick_sides(2, 3) * has_up, pick_sides(4, 5) * has_down
    corner_lane = iota((16, 128), 1)
    corners = jnp.where(corner_lane == 0, up[:, LL - 1 : LL], 0.0)
    corners = jnp.where(corner_lane == 1, down[:, 0:1], corners)
    corners = jnp.where(corner_lane == 2, up[:, TILES - 1 : TILES], corners)
    corners = jnp.where(corner_lane == 3, down[:, LL : LL + 1], corners)
    lines_of = jnp.concatenate([middle, corners], axis=1)
    lines_of = jnp.concatenate([lines_of, jnp.zeros((112, TILES + 128), F32)], axis=0).T.astype(BF16)
    pr, pc = iota((128, 128), 0), iota((128, 128), 1)
    for c in range(6):
        place = jnp.where(((pr == 8 + c) & (pc == 0)) | ((pr == c) & (pc == 127)), 1.0, 0.0).astype(BF16)
        placed = dot(lines_of, place)
        pbuf[c, TOP_L : TOP_L + LL, :] = placed[0:LL]
        pbuf[c, TOP_S : TOP_S + LS, :] = placed[LL:TILES]
        pbuf[c, TOP_L - 1 : TOP_L, :] = placed[TILES : TILES + 1]
        pbuf[c, TOP_L + LL : TOP_L + LL + 1, :] = placed[TILES + 1 : TILES + 2]
        pbuf[c, TOP_S - 1 : TOP_S, :] = placed[TILES + 2 : TILES + 3]
        pbuf[c, TOP_S + LS : TOP_S + LS + 1, :] = placed[TILES + 3 : TILES + 4]
        for top, lines, first in ((TOP_L, LL, 0), (TOP_S, LS, 6)):
            xbuf[c, top - 1 : top, :] = hrows[0, first + c].astype(F32)[15:16] * has_up
            xbuf[c, top + lines : top + lines + 1, :] = hrows[1, first + c].astype(F32)[0:1] * has_down

    lane80 = iota((80, 128), 1)

    def beside_lanes(x, p):
        return (
            jnp.where(lane80 == 0, p, pltpu.roll(x, 1, 1)),
            jnp.where(lane80 == 127, p, pltpu.roll(x, 127, 1)),
        )

    def lines_three(h):
        return (pltpu.roll(h, 1, 0)[8:72], h[8:72], pltpu.roll(h, 79, 0)[8:72])

    def filter_chunk(i, _):
        base = pl.multiple_of(i * 64 + jnp.where(i >= LL // 64, 16, 0), 8)
        tile = i * 64
        power = jnp.zeros((80, 128), F32)
        placed_power = jnp.zeros((80, 128), F32)
        for c in range(6):
            x, p = xbuf[c, pl.ds(base, 80), :], pbuf[c, pl.ds(base, 80), :]
            power = power + x * x
            placed_power = placed_power + p * p
        nine = []
        for part in (power, *beside_lanes(power, placed_power)):
            nine.extend(lines_three(part))
        mean_power = sum(nine[1:], nine[0]) / 9.0
        spread = jnp.zeros((64, 128), F32)
        for part in nine:
            spread = spread + (part - mean_power) ** 2
        spread = spread / 9.0
        gain = spread / (spread + 0.25 * mean_power * mean_power + 1.0)
        for c in range(6):
            x, p = xbuf[c, pl.ds(base, 80), :], pbuf[c, pl.ds(base, 80), :]
            left, right = beside_lanes(x, p)
            a, b, d = lines_three(left + x + right)
            local_mean = (a + b + d) / 9.0
            filtered = local_mean + gain * (x[8:72] - local_mean)
            fflat[pl.ds(tile * 8 + c, 64, stride=8), :] = filtered.astype(BF16).astype(F32)
        return 0

    lax.fori_loop(0, TILES // 64, filter_chunk, 0)

    for copy in w_copies:
        copy.wait()

    code_lane = iota((128, 256), 1)
    r = lax.rem(code_lane, 32)
    code = jnp.where(r < 3 * CAP, lax.div(lax.rem(code_lane, 128), 64) * 16 + lax.rem(r, CAP), -1)

    def block_copy(dst, peer_dst, sem):
        return pltpu.make_async_remote_copy(
            src_ref=payload.at[peer_dst], dst_ref=recv.at[dst], send_sem=send_sem, recv_sem=recv_sem.at[sem],
            device_id=(lax.div(peer_dst, N_SWATH), lax.rem(peer_dst, N_SWATH)), device_id_type=MESH,
        )

    def send_group(i, _):
        first = lax.rem(me + i * 13, DEVICES // 4) * 4
        for j in range(4):
            for k in range(CAP):
                v = fbuf[source[k, first + j]]
                vbuf[pl.ds(j * 64 + k, 3, stride=CAP), :] = v[0:3]
                vbuf[pl.ds(j * 64 + 32 + k, 3, stride=CAP), :] = v[3:6]
        v = vbuf[...].astype(BF16)
        zero = jnp.zeros((128, 128), BF16)
        rhs = jnp.concatenate(
            [jnp.concatenate([v[0:128], zero], axis=1), jnp.concatenate([zero, v[128:256]], axis=1)], axis=0
        )
        total = jnp.zeros((128, 256), F32)
        for jj in range(2):
            pairs = []
            for k in range(CAP):
                wa = wbuf[jnp.minimum(source[k, first + jj], TILES - 1)]
                wb = wbuf[jnp.minimum(source[k, first + 2 + jj], TILES - 1)]
                pairs.append(jnp.concatenate([wa, wb], axis=1))
            out = dot(jnp.concatenate(pairs, axis=0), rhs, NT)
            for k in range(CAP):
                total = jnp.where(code == jj * 16 + k, out[k * 128 : (k + 1) * 128], total)
        stage[0:128] = total[:, 0:128].T
        stage[128:256] = total[:, 128:256].T
        for j in range(4):
            o = first + j
            stage[j * 64 + MARK_ROW : j * 64 + MARK_ROW + 1, :] = marks[pl.ds(o, 1), :]
            payload[o] = stage[j * 64 : (j + 1) * 64, :].astype(BF16)
        for j in range(4):
            o = first + j

            @pl.when(o != me)
            def _():
                block_copy(me, o, me).start()

        return 0

    lax.fori_loop(0, DEVICES // 4, send_group, 0)
    own = pltpu.make_async_copy(payload.at[me], recv.at[me], recv_sem.at[me])
    own.start()

    lane = iota((1, 128), 1)
    line_row = iota((LS, 128), 0).astype(F32)

    def take_group(i, _):
        first = lax.rem(lax.div(me, 8) + i, DEVICES // 8) * 8
        for j in range(8):
            pltpu.make_async_copy(payload.at[0], recv.at[first + j], recv_sem.at[first + j]).wait()
        hot = []
        for q in range(2):
            line = jnp.zeros((1, 128), F32)
            for j in range(4):
                part = recv[first + q * 4 + j, 16:32, :].astype(F32)[MARK_ROW - 16 : MARK_ROW - 15]
                line = jnp.where(lax.div(lane, 32) == j, part, line)
            hot.append(jnp.where(line_row == line, 1.0, 0.0).astype(BF16))
        hot = jnp.concatenate(hot, axis=1)
        for h in range(2):
            block = recv[pl.ds(first, 8), h * 32 : (h + 1) * 32, :].reshape(256, 128)
            wide = jnp.concatenate([block * maskbuf[n] for n in range(6)], axis=1)
            map_ref[h] = map_ref[h] + dot(hot, wide)
        return 0

    lax.fori_loop(0, DEVICES // 8, take_group, 0)

    pr, pc = iota((128, 128), 0), iota((128, 128), 1)
    packed = jnp.zeros((LS, 128), F32)
    for n in range(12):
        z = map_ref[n // 6, :, (n % 6) * 128 : (n % 6 + 1) * 128]
        pick = jnp.where(((pr == 0) & (pc == n)) | ((pr == 127) & (pc == 16 + n)), 1.0, 0.0).astype(BF16)
        big = z.astype(BF16)
        rest = z - big.astype(F32)
        mid = rest.astype(BF16)
        small = (rest - mid.astype(F32)).astype(BF16)
        packed = packed + (dot(big, pick) + dot(mid, pick) + dot(small, pick))
        zrows[n : n + 1, :] = z[0:1]
        zrows[16 + n : 17 + n, :] = z[LS - 1 : LS]
    for n in range(12, 16):
        zrows[n : n + 1, :] = jnp.zeros((1, 128), F32)
        zrows[16 + n : 17 + n, :] = jnp.zeros((1, 128), F32)
    zedge[...] = packed.T[0:32]

    last = around(zedge, cols_ref, es_sem, er_sem)
    n = len(AROUND)
    for side_n, ds in enumerate((1, -1)):
        last.append(
            pltpu.make_async_remote_copy(
                src_ref=zrows, dst_ref=rows_ref.at[side_n], send_sem=es_sem.at[n], recv_sem=er_sem.at[n],
                device_id=beside(ds, 0), device_id_type=MESH,
            )
        )
        n += 1
    for copy in last:
        copy.start()
    for copy in last:
        copy.wait()
    pltpu.make_async_copy(payload.at[pl.ds(0, DEVICES - 1)], payload.at[pl.ds(0, DEVICES - 1)], send_sem).wait()


def fit_kernel(map_ref, cols_ref, rows_ref, fit_ref, out_ref, zplace, ztop, gbuf):
    sec, swath = lax.axis_index("sec"), lax.axis_index("swath")
    has_up, has_down = flag(sec > 0), flag(sec < N_SEC - 1)
    has_left, has_right = flag(swath > 0), flag(swath < N_SWATH - 1)
    low = iota((32, LS), 0) < 16
    side = jnp.where(low, has_right, has_left)

    def pick_sides(left_n, right_n):
        return jnp.where(low, cols_ref[right_n], cols_ref[left_n]) * side

    middle = pick_sides(0, 1)
    up, down = pick_sides(2, 3) * has_up, pick_sides(4, 5) * has_down
    corner_lane = iota((32, 128), 1)
    corners = jnp.where(corner_lane == 0, up[:, LS - 1 : LS], 0.0)
    corners = jnp.where(corner_lane == 1, down[:, 0:1], corners)
    lines_of = jnp.concatenate([middle, corners], axis=1)
    lines_of = jnp.concatenate([lines_of, jnp.zeros((96, LS + 128), F32)], axis=0).T
    big = lines_of.astype(BF16)
    rest = lines_of - big.astype(F32)
    mid = rest.astype(BF16)
    small = (rest - mid.astype(F32)).astype(BF16)
    pr, pc = iota((128, 128), 0), iota((128, 128), 1)
    for n in range(12):
        place = jnp.where(((pr == 16 + n) & (pc == 0)) | ((pr == n) & (pc == 127)), 1.0, 0.0).astype(BF16)
        placed = dot(big, place) + dot(mid, place) + dot(small, place)
        zplace[n, 0:LS] = placed[0:LS]
        zplace[n, LS : LS + 8] = placed[LS : LS + 8]
        ztop[n, 0:1] = rows_ref[0, 16 + n : 17 + n] * has_up
        ztop[n, 1:2] = rows_ref[1, n : n + 1] * has_down
        ztop[n, 2:8] = jnp.zeros((6, 128), F32)

    lane = iota((8, 128), 1)
    matrix = fit_ref[...]

    def block(z):
        parts = [z[i] * z[j] + z[6 + i] * z[6 + j] for i, j in upper_pairs]
        parts += [z[6 + i] * z[j] - z[i] * z[6 + j] for i, j in strict_pairs]
        joint = jnp.concatenate(parts, axis=0)
        high = joint.astype(BF16)
        rest_ = (joint - high.astype(F32)).astype(BF16)
        first = dot(matrix, high)
        g = first[0:128] + first[128:256] + dot(matrix[0:128], rest_)
        sums = []
        for k in range(16):
            g1, g2 = g[k * 8 : k * 8 + 8, 0:128], g[k * 8 : k * 8 + 8, 128:256]
            left = jnp.where(lane == 0, g2, pltpu.roll(g1, 1, 1))
            right = jnp.where(lane == 127, g2, pltpu.roll(g1, 127, 1))
            sums.append(left + g1 + right)
        return sums

    def step(b, _):
        at = pl.multiple_of(b * 8, 8)
        z = [
            jnp.concatenate(
                [
                    map_ref[n // 6, pl.ds(at, 8), (n % 6) * 128 : (n % 6 + 1) * 128],
                    zplace[n, pl.ds(at, 8), :],
                ],
                axis=1,
            )
            for n in range(12)
        ]
        for k, s in enumerate(block(z)):
            gbuf[k, pl.ds(at + 8, 8), :] = s
        return 0

    lax.fori_loop(0, LS // 8, step, 0)
    z = [jnp.concatenate([ztop[n], zplace[n, LS : LS + 8]], axis=1) for n in range(12)]
    for k, s in enumerate(block(z)):
        gbuf[k, 7:8, :] = s[0:1]
        gbuf[k, LS + 8 : LS + 9, :] = s[1:2]
    for k in range(16):
        out_ref[k] = gbuf[k, 7 : 7 + LS] + gbuf[k, 8 : 8 + LS] + gbuf[k, 9 : 9 + LS]


def vmem(n=1):
    return [pl.BlockSpec(memory_space=pltpu.VMEM)] * n


def body(radar_l, radar_s, weights_l, weights_s, owner_l, owner_s, slot_l, slot_s, models):
    source, marks, matrix = pl.pallas_call(
        plan_kernel,
        out_shape=(
            jax.ShapeDtypeStruct((16, DEVICES), I32),
            jax.ShapeDtypeStruct((DEVICES, 128), F32),
            jax.ShapeDtypeStruct((256, NJ * 8), BF16),
        ),
        in_specs=vmem(5),
        out_specs=vmem(3),
        compiler_params=pltpu.CompilerParams(vmem_limit_bytes=32 << 20),
        name="plan",
    )(owner_l, owner_s, slot_l.reshape(1, LL), slot_s.reshape(1, LS), models)
    dma, n_around = pltpu.SemaphoreType.DMA, len(AROUND)
    maps, cols, rows = pl.pallas_call(
        main_kernel,
        out_shape=(
            jax.ShapeDtypeStruct((2, LS, 768), F32),
            jax.ShapeDtypeStruct((n_around, 32, LS), F32),
            jax.ShapeDtypeStruct((2, 32, 128), F32),
        ),
        in_specs=vmem(2)
        + [pl.BlockSpec(memory_space=pl.ANY)] * 2
        + [pl.BlockSpec(memory_space=pltpu.SMEM)]
        + vmem(1),
        out_specs=vmem(3),
        scratch_shapes=[
            pltpu.VMEM((TILES, 128, 128), BF16),
            pltpu.VMEM((6, EXT, 128), F32),
            pltpu.VMEM((6, EXT, 128), F32),
            pltpu.VMEM((TILES + 1, 8, 128), F32),
            pltpu.VMEM((256, 128), F32),
            pltpu.VMEM((256, 128), F32),
            pltpu.VMEM((DEVICES, ROWS, 128), BF16),
            pltpu.VMEM((DEVICES, ROWS, 128), BF16),
            pltpu.VMEM((6, 256, 128), BF16),
            pltpu.VMEM((16, TILES), BF16),
            pltpu.VMEM((n_around, 16, TILES), BF16),
            pltpu.VMEM((2, 12, 16, 128), BF16),
            pltpu.VMEM((32, LS), F32),
            pltpu.VMEM((32, 128), F32),
            dma((8,)),
            dma((n_around + 4,)),
            dma((n_around + 4,)),
            dma,
            dma((DEVICES,)),
            dma((n_around + 2,)),
            dma((n_around + 2,)),
        ],
        compiler_params=pltpu.CompilerParams(
            collective_id=0, has_side_effects=True, vmem_limit_bytes=56 << 20
        ),
        name="unite",
    )(radar_l, radar_s, weights_l, weights_s, source, marks)
    return pl.pallas_call(
        fit_kernel,
        out_shape=jax.ShapeDtypeStruct((16, LS, 128), F32),
        in_specs=vmem(4),
        out_specs=vmem(1)[0],
        scratch_shapes=[
            pltpu.VMEM((12, LS + 8, 128), F32),
            pltpu.VMEM((12, 8, 128), F32),
            pltpu.VMEM((16, LS + 16, 128), F32),
        ],
        compiler_params=pltpu.CompilerParams(vmem_limit_bytes=32 << 20),
        name="fit",
    )(maps, cols, rows, matrix)


def solution(mesh):
    in_specs = (
        P(None, "sec", "swath"),
        P(None, "sec", "swath"),
        P(("sec", "swath"), None, None),
        P(("sec", "swath"), None, None),
        P(("sec", "swath"), None),
        P(("sec", "swath"), None),
        P(("sec", "swath")),
        P(("sec", "swath")),
        P(),
    )
    out_specs = P(None, "sec", "swath")
    return jax.shard_map(body, mesh=mesh, in_specs=in_specs, out_specs=out_specs, check_vma=False)
```

time: 288 us -> 94.5 us (0.33)
  the two profiles are of different devices: /device:TPU:9 before, /device:TPU:1 now
where the time goes in v1:
time: 94.5 us; the launch traced here: 93.9 us
  Pallas kernels  85.9 us (91%)
  local copies, waits for them, and re-layouts  7.98 us (8%)
    pallas_call x1, Pallas kernels, body(): pl.pallas_call(main_kernel, out_shape=(jax.ShapeDtypeStruct((2, LS, 768),...  70.3 us
    pallas_call x1, Pallas kernels, body(): pl.pallas_call(fit_kernel, out_shape=jax.ShapeDtypeStruct((16, LS, 128),...  13.7 us
    unnamed x16, local copies, waits for them, and re-layouts  7.3 us
    pallas_call x1, Pallas kernels, body(): pl.pallas_call(plan_kernel, out_shape=(jax.ShapeDtypeStruct((16, DEVICES)...  1.92 us

profile of v1, /device:TPU:1, one launch (start us, length us, event | category | flops | bytes accessed | tf_op | source)
XLA Modules:
  0.0 93.9 jit_solution(1777780578312681167)
XLA Ops:
  0.0 0.7 reshape.6.slot_l
  0.7 0.8 copy.11.owner_s
  1.5 0.8 copy.10.owner_l
  2.3 0.0 copy-start.5
  2.3 0.7 copy-done.5
  3.0 0.0 copy-start.6
  3.0 0.7 copy-done.6
  3.7 1.9 %plan.1 = (s32[16,128]{1,0:T(8,128)S(1)}, f32[128,128]{1,0:T(8,128)S(1)}, bf16[256,288]{1,0:T(8,128)(2,1)S(1)}) custom-call(s32[384,1]{1,0:T(8,128)S(1)} %copy.10.owner_l, s32[256,1]{1,0:T(8,128)S(1)} %copy.11.owner_s, s32[1,384]{1,0:T(1,128)S(1)} %reshape.6.slot_l, s32[1,256]{1,0:T(1,128)S(1)} %bitcast.1, f32[16,36]{1,0:T(8,128)S(1)} %copy-done.5), custom_call_target="tpu_custom_call" | custom-call | tf_op jit(solution)/shard_map/plan/pallas_call | solution.py:447
  5.6 0.0 copy-start.2
  5.6 0.6 copy-done.2
  6.3 0.0 copy-start.4
  6.3 0.6 copy-done.4
  6.9 70.3 %unite.1 = (f32[2,256,768]{2,1,0:T(8,128)}, f32[6,32,256]{2,1,0:T(8,128)}, f32[2,32,128]{2,1,0:T(8,128)}) custom-call(bf16[6,384,128]{2,1,0:T(8,128)(2,1)} %radar_l.1, bf16[6,256,128]{2,1,0:T(8,128)(2,1)} %radar_s.1, bf16[384,128,128]{2,1,0:T(8,128)(2,1)} %weights_l.1, bf16[256,128,128]{2,1,0:T(8,128)(2,1)} %weights_s.1, s32[16,128]{1,0:T(8,128)} %copy-done.4, ...), custom_call_target="tpu_custom_call" | custom-call | tf_op jit(solution)/shard_map/unite/pallas_call | solution.py:460
  77.1 0.0 copy-start
  77.1 1.4 %copy-done = f32[2,256,768]{2,1,0:T(8,128)S(1)} copy-done((f32[2,256,768]{2,1,0:T(8,128)S(1)}, f32[2,256,768]{2,1,0:T(8,128)}, u32[]{:S(2)}) %copy-start) | copy-done | bytes 1572888
  78.5 0.0 copy-start.1
  78.5 0.9 copy-done.1
  79.5 0.0 copy-start.3
  79.5 0.8 copy-done.3
  80.2 13.7 %fit.1 = f32[16,256,128]{2,1,0:T(8,128)} custom-call(f32[2,256,768]{2,1,0:T(8,128)S(1)} %copy-done, f32[6,32,256]{2,1,0:T(8,128)S(1)} %copy-done.1, f32[2,32,128]{2,1,0:T(8,128)S(1)} %copy-done.3, bf16[256,288]{1,0:T(8,128)(2,1)S(1)} %get-tuple-element.16.fit_ref), custom_call_target="tpu_custom_call" | custom-call | tf_op jit(solution)/shard_map/fit/pallas_call | solution.py:500
Async XLA Ops:
  2.3 0.7 copy-start.5
  3.0 0.7 copy-start.6
  5.6 0.6 copy-start.2
  6.3 0.6 copy-start.4
  77.1 1.4 %copy-start = (f32[2,256,768]{2,1,0:T(8,128)S(1)}, f32[2,256,768]{2,1,0:T(8,128)}, u32[]{:S(2)}) copy-start(f32[2,256,768]{2,1,0:T(8,128)} %get-tuple-element.13.map_ref) | copy-start | bytes 4718596
  78.5 0.9 copy-start.1
  79.5 0.8 copy-start.3

commit v2 on v1

v2 whole, which is shorter than its diff:
```python
import functools

import jax
import jax.numpy as jnp
from jax import lax
from jax.experimental import pallas as pl
from jax.experimental.pallas import tpu as pltpu
from jax.sharding import PartitionSpec as P

MESH = pl.DeviceIdType.MESH
F32, BF16, I32 = jnp.float32, jnp.bfloat16, jnp.int32
FIT_ITERS = 4
FIT_RATE = 0.25
N_SEC, N_SWATH, DEVICES = 4, 32, 128
LL, LS = 384, 256
CAP_L, CAP_S = 6, 4
CAP = CAP_L + CAP_S
TILES = LL + LS
ROWS = 64
MARK_ROW = 30
TOP_L, TOP_S = 8, 8 + LL + 16
EXT = LL + LS + 32
upper_pairs = [(i, j) for i in range(6) for j in range(i, 6)]
strict_pairs = [(i, j) for i in range(6) for j in range(i + 1, 6)]
NJ = len(upper_pairs) + len(strict_pairs)
AROUND = [(0, -1), (0, 1), (-1, -1), (-1, 1), (1, -1), (1, 1)]


def iota(shape, dim):
    return lax.broadcasted_iota(I32, shape, dim)


def dot(a, b, dims=((1,), (0,)), precision=None):
    return lax.dot_general(a, b, (dims, ((), ())), precision=precision, preferred_element_type=F32)


NT = ((1,), (1,))


def flag(cond):
    return jnp.where(cond, 1.0, 0.0).astype(F32)


def fill_plan(owner_l, owner_s, slot_l, slot_s, source_ref, marks_ref):
    rows, marks = [], []
    for owner, slot, lines, cap, first in ((owner_l, slot_l, LL, CAP_L, 0), (owner_s, slot_s, LS, CAP_S, LL)):
        hit = jnp.where(owner[...] == iota((DEVICES, lines), 0), 1.0, 0.0).astype(F32)
        earlier = jnp.where(iota((lines, lines), 0) < iota((lines, lines), 1), 1.0, 0.0).astype(BF16)
        before = dot(hit.astype(BF16), earlier)
        tile = iota((1, lines), 1) + first
        facts = jnp.concatenate(
            [
                slot[...].astype(F32),
                lax.rem(tile, 128).astype(F32),
                lax.div(tile, 128).astype(F32),
                jnp.ones((1, lines), F32),
                jnp.zeros((4, lines), F32),
            ],
            axis=0,
        ).astype(BF16)
        for k in range(cap):
            got = dot(facts, jnp.where(before == k, hit, 0.0).astype(BF16), NT)
            filled = got[3:4]
            rows.append(got[1:2] + 128.0 * got[2:3] + (1.0 - filled) * TILES)
            marks.append(got[0:1] + filled - 1.0)
    tiles = jnp.concatenate(rows + [jnp.zeros((16 - CAP, DEVICES), F32)], axis=0).astype(I32)
    source_ref[...] = jnp.clip(tiles, 0, TILES)
    table = jnp.concatenate(marks + [jnp.zeros((DEVICES - CAP, DEVICES), F32)], axis=0)
    lane = lax.rem(iota((DEVICES, 128), 1), 32)
    spread = jnp.where((lax.rem(lane, CAP) == iota((DEVICES, 128), 0)) & (lane < 3 * CAP), 1.0, 0.0).astype(BF16)
    marks_ref[...] = dot(table.T.astype(BF16), spread) - jnp.where(lane < 3 * CAP, 0.0, 1.0)


def fill_matrix(models, matrix_ref):
    high = lax.Precision.HIGHEST
    m = models[...]
    gram = dot(m, m, NT, precision=high)
    total = m
    for _ in range(FIT_ITERS - 1):
        total = m + total - FIT_RATE * dot(gram, total, precision=high)
    total = total * (FIT_RATE / 9.0)
    left = jnp.where(lax.div(iota((128, 16), 0), 8) == iota((128, 16), 1), 1.0, 0.0).astype(F32)
    right = jnp.where(lax.div(iota((NJ, NJ * 8), 1), 8) == iota((NJ, NJ * 8), 0), 1.0, 0.0).astype(F32)
    wide = dot(dot(left, total, precision=high), right, precision=high)
    same = lax.rem(iota((128, NJ * 8), 0), 8) == lax.rem(iota((128, NJ * 8), 1), 8)
    wide = jnp.where(same, wide, 0.0)
    big = wide.astype(BF16)
    matrix_ref[0:128] = big
    matrix_ref[128:256] = (wide - big.astype(F32)).astype(BF16)


def halves(x):
    big = x.astype(BF16)
    return jnp.concatenate([big, (x - big.astype(F32)).astype(BF16)], axis=1)


def joint_of(z):
    parts = [z[i] * z[j] + z[6 + i] * z[6 + j] for i, j in upper_pairs]
    parts += [z[6 + i] * z[j] - z[i] * z[6 + j] for i, j in strict_pairs]
    return jnp.concatenate(parts, axis=0)


def main_kernel(
    radar_l_hbm, radar_s_hbm, weights_l, weights_s, owner_l_hbm, owner_s_hbm, slot_l_hbm, slot_s_hbm, models_hbm,
    out_ref,
    radar_l, radar_s, owner_l, owner_s, slot_l, slot_s, models,
    wbuf, xbuf, pbuf, fbuf, vbuf, stage, payload, recv, maskbuf, edge, hcols, hrows,
    source_v, source, marks, matrix, zmap, zedge, zrows, zcols_in, zrows_in, zv, gbuf, gv, hbuf, halo_lines, obuf,
    in_sem, w_sem, hs_sem, hr_sem, send_sem, recv_sem, es_sem, er_sem, plan_sem, out_sem,
):
    sec, swath = lax.axis_index("sec"), lax.axis_index("swath")
    me = sec * N_SWATH + swath
    my_place = swath * N_SEC + sec

    pairs = (
        (radar_l_hbm, radar_l), (radar_s_hbm, radar_s), (owner_l_hbm, owner_l), (owner_s_hbm, owner_s),
        (slot_l_hbm, slot_l), (slot_s_hbm, slot_s), (models_hbm, models),
    )
    loads = [pltpu.make_async_copy(a, b, in_sem.at[n]) for n, (a, b) in enumerate(pairs)]
    for copy in loads:
        copy.start()

    barrier = pltpu.get_barrier_semaphore()

    def greet(i, _):
        peer = lax.rem(me + i, DEVICES)
        pl.semaphore_signal(
            barrier, inc=1, device_id=(lax.div(peer, N_SWATH), lax.rem(peer, N_SWATH)), device_id_type=MESH
        )
        return 0

    lax.fori_loop(1, DEVICES, greet, 0)
    for copy in loads:
        copy.wait()

    column, row = iota((16, 128), 1), iota((16, 128), 0)
    for radar, first, lines in ((radar_l, 0, LL), (radar_s, LL, LS)):
        total = jnp.zeros((16, lines), F32)
        for c in range(6):
            pick = jnp.where(
                ((row == c) & (column == 0)) | ((row == 8 + c) & (column == 127)), 1.0, 0.0
            ).astype(BF16)
            total = total + dot(pick, radar[c], NT)
        edge[:, first : first + lines] = total.astype(BF16)

    pl.semaphore_wait(barrier, DEVICES - 1)

    def beside(ds, dw):
        return (lax.rem(sec + ds + N_SEC, N_SEC), lax.rem(swath + dw + N_SWATH, N_SWATH))

    def around(src, slots, ssem, rsem):
        return [
            pltpu.make_async_remote_copy(
                src_ref=src, dst_ref=slots.at[n], send_sem=ssem.at[n], recv_sem=rsem.at[n],
                device_id=beside(-ds, -dw), device_id_type=MESH,
            )
            for n, (ds, dw) in enumerate(AROUND)
        ]

    halo = around(edge, hcols, hs_sem, hr_sem)
    n = len(AROUND)
    for radar, first, lines in ((radar_l, 0, LL), (radar_s, 6, LS)):
        for side, (start, ds) in enumerate(((lines - 16, 1), (0, -1))):
            halo.append(
                pltpu.make_async_remote_copy(
                    src_ref=radar.at[:, pl.ds(start, 16), :],
                    dst_ref=hrows.at[side, pl.ds(first, 6)],
                    send_sem=hs_sem.at[n], recv_sem=hr_sem.at[n],
                    device_id=beside(ds, 0), device_id_type=MESH,
                )
            )
            n += 1
    for copy in halo:
        copy.start()

    w_copies = []
    for n, (src, first, count) in enumerate(((weights_l, 0, LL), (weights_s, LL, LS))):
        for part in range(4):
            size = count // 4
            w_copies.append(
                pltpu.make_async_copy(
                    src.at[pl.ds(part * size, size)],
                    wbuf.at[pl.ds(first + part * size, size)],
                    w_sem.at[4 * n + part],
                )
            )
    for copy in w_copies:
        copy.start()

    fill_plan(owner_l, owner_s, slot_l, slot_s, source_v, marks)
    plan_copy = pltpu.make_async_copy(source_v, source, plan_sem)
    plan_copy.start()
    for radar, top, lines in ((radar_l, TOP_L, LL), (radar_s, TOP_S, LS)):
        for c in range(6):
            xbuf[c, top : top + lines, :] = radar[c].astype(F32)
    fbuf[TILES] = jnp.zeros((8, 128), F32)
    fflat = fbuf.reshape((TILES + 1) * 8, 128)
    vbuf[...] = jnp.zeros((256, 128), F32)
    zmap[...] = jnp.zeros((2, LS, 768), F32)
    r32 = lax.rem(iota((256, 128), 0), 32)
    for band in range(2):
        for c in range(3):
            k = r32 - 10 * c
            keep = (k >= 0) & (k < CAP_L) if band == 0 else (k >= CAP_L) & (k < CAP)
            maskbuf[band * 3 + c] = jnp.where(keep, 1.0, 0.0).astype(BF16)
    fill_matrix(models, matrix)

    for copy in halo:
        copy.wait()

    has_up, has_down = flag(sec > 0), flag(sec < N_SEC - 1)
    has_left, has_right = flag(swath > 0), flag(swath < N_SWATH - 1)
    low = iota((16, TILES), 0) < 8
    side = jnp.where(low, has_right, has_left)

    def pick_sides(left_n, right_n):
        return jnp.where(low, hcols[right_n].astype(F32), hcols[left_n].astype(F32)) * side

    middle = pick_sides(0, 1)
    up, down = pick_sides(2, 3) * has_up, pick_sides(4, 5) * has_down
    corner_lane = iota((16, 128), 1)
    corners = jnp.where(corner_lane == 0, up[:, LL - 1 : LL], 0.0)
    corners = jnp.where(corner_lane == 1, down[:, 0:1], corners)
    corners = jnp.where(corner_lane == 2, up[:, TILES - 1 : TILES], corners)
    corners = jnp.where(corner_lane == 3, down[:, LL : LL + 1], corners)
    lines_of = jnp.concatenate([middle, corners], axis=1)
    lines_of = jnp.concatenate([lines_of, jnp.zeros((112, TILES + 128), F32)], axis=0).T.astype(BF16)
    pr, pc = iota((128, 128), 0), iota((128, 128), 1)
    for c in range(6):
        place = jnp.where(((pr == 8 + c) & (pc == 0)) | ((pr == c) & (pc == 127)), 1.0, 0.0).astype(BF16)
        placed = dot(lines_of, place)
        pbuf[c, TOP_L : TOP_L + LL, :] = placed[0:LL]
        pbuf[c, TOP_S : TOP_S + LS, :] = placed[LL:TILES]
        pbuf[c, TOP_L - 1 : TOP_L, :] = placed[TILES : TILES + 1]
        pbuf[c, TOP_L + LL : TOP_L + LL + 1, :] = placed[TILES + 1 : TILES + 2]
        pbuf[c, TOP_S - 1 : TOP_S, :] = placed[TILES + 2 : TILES + 3]
        pbuf[c, TOP_S + LS : TOP_S + LS + 1, :] = placed[TILES + 3 : TILES + 4]
        for top, lines, first in ((TOP_L, LL, 0), (TOP_S, LS, 6)):
            xbuf[c, top - 1 : top, :] = hrows[0, first + c].astype(F32)[15:16] * has_up
            xbuf[c, top + lines : top + lines + 1, :] = hrows[1, first + c].astype(F32)[0:1] * has_down

    def beside_lanes(x, p):
        lane = iota(x.shape, 1)
        return (
            jnp.where(lane == 0, p, pltpu.roll(x, 1, 1)),
            jnp.where(lane == 127, p, pltpu.roll(x, 127, 1)),
        )

    def lines_three(h):
        return (pltpu.roll(h, 1, 0)[8:72], h[8:72], pltpu.roll(h, 79, 0)[8:72])

    def filter_chunk(i, _):
        base = pl.multiple_of(i * 64 + jnp.where(i >= LL // 64, 16, 0), 8)
        tile = i * 64
        power = jnp.zeros((80, 128), F32)
        placed_power = jnp.zeros((80, 128), F32)
        for c in range(6):
            x, p = xbuf[c, pl.ds(base, 80), :], pbuf[c, pl.ds(base, 80), :]
            power = power + x * x
            placed_power = placed_power + p * p
        nine = []
        for part in (power, *beside_lanes(power, placed_power)):
            nine.extend(lines_three(part))
        mean_power = sum(nine[1:], nine[0]) / 9.0
        spread = jnp.zeros((64, 128), F32)
        for part in nine:
            spread = spread + (part - mean_power) ** 2
        spread = spread / 9.0
        gain = spread / (spread + 0.25 * mean_power * mean_power + 1.0)
        for c in range(6):
            x, p = xbuf[c, pl.ds(base, 80), :], pbuf[c, pl.ds(base, 80), :]
            left, right = beside_lanes(x, p)
            a, b, d = lines_three(left + x + right)
            local_mean = (a + b + d) / 9.0
            filtered = local_mean + gain * (x[8:72] - local_mean)
            fflat[pl.ds(tile * 8 + c, 64, stride=8), :] = filtered.astype(BF16).astype(F32)
        return 0

    lax.fori_loop(0, TILES // 64, filter_chunk, 0)

    plan_copy.wait()
    for copy in w_copies:
        copy.wait()

    code_lane = iota((128, 256), 1)
    r = lax.rem(code_lane, 32)
    code = jnp.where(r < 3 * CAP, lax.div(lax.rem(code_lane, 128), 64) * 16 + lax.rem(r, CAP), -1)

    def send_group(i, _):
        first = lax.rem(swath + i * 13, DEVICES // 4) * 4
        for j in range(4):
            for k in range(CAP):
                v = fbuf[source[k, first + j]]
                vbuf[pl.ds(j * 64 + k, 3, stride=CAP), :] = v[0:3]
                vbuf[pl.ds(j * 64 + 32 + k, 3, stride=CAP), :] = v[3:6]
        v = vbuf[...].astype(BF16)
        zero = jnp.zeros((128, 128), BF16)
        rhs = jnp.concatenate(
            [jnp.concatenate([v[0:128], zero], axis=1), jnp.concatenate([zero, v[128:256]], axis=1)], axis=0
        )
        total = jnp.zeros((128, 256), F32)
        for jj in range(2):
            both = []
            for k in range(CAP):
                wa = wbuf[jnp.minimum(source[k, first + jj], TILES - 1)]
                wb = wbuf[jnp.minimum(source[k, first + 2 + jj], TILES - 1)]
                both.append(jnp.concatenate([wa, wb], axis=1))
            out = dot(jnp.concatenate(both, axis=0), rhs, NT)
            for k in range(CAP):
                total = jnp.where(code == jj * 16 + k, out[k * 128 : (k + 1) * 128], total)
        stage[0:128] = total[:, 0:128].T
        stage[128:256] = total[:, 128:256].T
        for j in range(4):
            o = first + j
            stage[j * 64 + MARK_ROW : j * 64 + MARK_ROW + 1, :] = marks[pl.ds(o, 1), :]
            payload[o] = stage[j * 64 : (j + 1) * 64, :].astype(BF16)
        for j in range(4):
            o = first + j

            @pl.when(o != me)
            def _():
                pltpu.make_async_remote_copy(
                    src_ref=payload.at[o], dst_ref=recv.at[my_place], send_sem=send_sem, recv_sem=recv_sem.at[my_place],
                    device_id=(lax.div(o, N_SWATH), lax.rem(o, N_SWATH)), device_id_type=MESH,
                ).start()

        return 0

    lax.fori_loop(0, DEVICES // 4, send_group, 0)
    own = pltpu.make_async_copy(payload.at[me], recv.at[my_place], recv_sem.at[my_place])
    own.start()

    mark_lane = iota((1, 128), 1)
    line_row = iota((LS, 128), 0).astype(F32)
    my_group = lax.div(me, 4)

    def take_group(i, _):
        starts = [
            pl.multiple_of(lax.rem(my_group + (2 * i + q) * 19, N_SWATH) * N_SEC, N_SEC) for q in range(2)
        ]
        hot = []
        for start in starts:
            for j in range(4):
                pltpu.make_async_copy(payload.at[0], recv.at[start + j], recv_sem.at[start + j]).wait()
        for start in starts:
            line = jnp.zeros((1, 128), F32)
            for j in range(4):
                part = recv[start + j, 16:32, :].astype(F32)[MARK_ROW - 16 : MARK_ROW - 15]
                line = jnp.where(lax.div(mark_lane, 32) == j, part, line)
            hot.append(jnp.where(line_row == line, 1.0, 0.0).astype(BF16))
        hot = jnp.concatenate(hot, axis=1)
        for h in range(2):
            block = jnp.concatenate(
                [recv[pl.ds(start, 4), h * 32 : (h + 1) * 32, :].reshape(128, 128) for start in starts], axis=0
            )
            wide = jnp.concatenate([block * maskbuf[n] for n in range(6)], axis=1)
            zmap[h] = zmap[h] + dot(hot, wide)
        return 0

    lax.fori_loop(0, DEVICES // 8, take_group, 0)

    packed = jnp.zeros((LS, 128), F32)
    qr, qc = lax.rem(iota((256, 128), 0), 128), iota((256, 128), 1)
    for n in range(12):
        z = zmap[n // 6, :, (n % 6) * 128 : (n % 6 + 1) * 128]
        pick = jnp.where(((qr == 0) & (qc == n)) | ((qr == 127) & (qc == 16 + n)), 1.0, 0.0).astype(BF16)
        packed = packed + dot(halves(z), pick)
        zrows[n : n + 1, :] = z[0:1]
        zrows[16 + n : 17 + n, :] = z[LS - 1 : LS]
    zrows[12:16, :] = jnp.zeros((4, 128), F32)
    zrows[28:32, :] = jnp.zeros((4, 128), F32)
    zedge[...] = packed.T[0:32]
    last = around(zedge, zcols_in, es_sem, er_sem)
    n = len(AROUND)
    for side_n, ds in enumerate((1, -1)):
        last.append(
            pltpu.make_async_remote_copy(
                src_ref=zrows, dst_ref=zrows_in.at[side_n], send_sem=es_sem.at[n], recv_sem=er_sem.at[n],
                device_id=beside(ds, 0), device_id_type=MESH,
            )
        )
        n += 1
    for copy in last:
        copy.start()

    def fit_lines(b, _):
        at = pl.multiple_of(b * 16, 16)
        both = []
        for part in range(2):
            z = [zmap[n // 6, pl.ds(at + part * 8, 8), (n % 6) * 128 : (n % 6 + 1) * 128] for n in range(12)]
            both.append(joint_of(z))
        g = dot(matrix[...], jnp.concatenate(both, axis=1).astype(BF16))
        g = g[0:128] + g[128:256]
        for k in range(16):
            gbuf[k, pl.ds(at, 8), :] = g[k * 8 : k * 8 + 8, 0:128]
            gbuf[k, pl.ds(at + 8, 8), :] = g[k * 8 : k * 8 + 8, 128:256]
        return 0

    lax.fori_loop(0, LS // 16, fit_lines, 0)

    for copy in last:
        copy.wait()

    low = iota((32, LS), 0) < 16
    side = jnp.where(low, has_right, has_left)

    def pick_map_sides(left_n, right_n):
        return jnp.where(low, zcols_in[right_n], zcols_in[left_n]) * side

    middle = pick_map_sides(0, 1)
    up, down = pick_map_sides(2, 3) * has_up, pick_map_sides(4, 5) * has_down
    corner_lane = iota((32, 128), 1)
    corners = jnp.where(lax.rem(corner_lane, 2) == 0, up[:, LS - 1 : LS], down[:, 0:1])
    for n in range(12):
        zv[n, 0:1] = middle[16 + n : 17 + n, 0:128]
        zv[n, 1:2] = middle[16 + n : 17 + n, 128:256]
        zv[n, 2:3] = middle[n : n + 1, 0:128]
        zv[n, 3:4] = middle[n : n + 1, 128:256]
        zv[n, 4:5] = jnp.where(mark_lane < 2, corners[16 + n : 17 + n], corners[n : n + 1])
        zv[n, 5:6] = zrows_in[0, 16 + n : 17 + n] * has_up
        zv[n, 6:7] = zrows_in[1, n : n + 1] * has_down
        zv[n, 7:8] = jnp.zeros((1, 128), F32)
    g = dot(matrix[...], joint_of([zv[n] for n in range(12)]).astype(BF16))
    g = g[0:128] + g[128:256]
    gv[...] = g
    corner = gv[pl.ds(4, 16, stride=8), :]
    lane16 = iota((16, 128), 1)
    for side_n in range(2):
        edge_line = gv[pl.ds(5 + side_n, 16, stride=8), :]
        left, right = corner[:, side_n : side_n + 1], corner[:, 2 + side_n : 3 + side_n]
        halo_lines[side_n] = (
            edge_line
            + jnp.where(lane16 == 0, left, pltpu.roll(edge_line, 1, 1))
            + jnp.where(lane16 == 127, right, pltpu.roll(edge_line, 127, 1))
        )
    turned = g.T
    turned = halves(jnp.concatenate([turned, pltpu.roll(turned, 127, 1)], axis=0))

    def finish(k, _):
        place = jnp.where(
            ((qr == k * 8) & (qc == 0)) | ((qr == k * 8 + 2) & (qc == 127)), 1.0, 0.0
        ).astype(BF16)
        beside_block = dot(turned, place)
        own_cells = gbuf[k]
        left, right = beside_lanes(own_cells, beside_block)
        hbuf[8 : 8 + LS] = own_cells + left + right
        hbuf[7:8] = halo_lines[0, pl.ds(k, 1), :]
        hbuf[8 + LS : 9 + LS] = halo_lines[1, pl.ds(k, 1), :]
        obuf[k] = hbuf[7 : 7 + LS] + hbuf[8 : 8 + LS] + hbuf[9 : 9 + LS]
        pltpu.make_async_copy(obuf.at[k], out_ref.at[k], out_sem.at[k]).start()
        return 0

    lax.fori_loop(0, 16, finish, 0)
    pltpu.make_async_copy(payload.at[pl.ds(0, DEVICES - 1)], payload.at[pl.ds(0, DEVICES - 1)], send_sem).wait()

    def written(k, _):
        pltpu.make_async_copy(obuf.at[k], out_ref.at[k], out_sem.at[k]).wait()
        return 0

    lax.fori_loop(0, 16, written, 0)


def body(radar_l, radar_s, weights_l, weights_s, owner_l, owner_s, slot_l, slot_s, models):
    dma, n_around = pltpu.SemaphoreType.DMA, len(AROUND)
    vmem = pltpu.VMEM
    return pl.pallas_call(
        main_kernel,
        out_shape=jax.ShapeDtypeStruct((16, LS, 128), F32),
        in_specs=[pl.BlockSpec(memory_space=pl.ANY)] * 9,
        out_specs=pl.BlockSpec(memory_space=pl.ANY),
        scratch_shapes=[
            vmem((6, LL, 128), BF16),
            vmem((6, LS, 128), BF16),
            vmem((1, LL), I32),
            vmem((1, LS), I32),
            vmem((1, LL), I32),
            vmem((1, LS), I32),
            vmem((16, NJ), F32),
            vmem((TILES, 128, 128), BF16),
            vmem((6, EXT, 128), F32),
            vmem((6, EXT, 128), F32),
            vmem((TILES + 1, 8, 128), F32),
            vmem((256, 128), F32),
            vmem((256, 128), F32),
            vmem((DEVICES, ROWS, 128), BF16),
            vmem((DEVICES, ROWS, 128), BF16),
            vmem((6, 256, 128), BF16),
            vmem((16, TILES), BF16),
            vmem((n_around, 16, TILES), BF16),
            vmem((2, 12, 16, 128), BF16),
            vmem((16, DEVICES), I32),
            pltpu.SMEM((16, DEVICES), I32),
            vmem((DEVICES, 128), F32),
            vmem((256, NJ * 8), BF16),
            vmem((2, LS, 768), F32),
            vmem((32, LS), F32),
            vmem((32, 128), F32),
            vmem((n_around, 32, LS), F32),
            vmem((2, 32, 128), F32),
            vmem((12, 8, 128), F32),
            vmem((16, LS, 128), F32),
            vmem((128, 128), F32),
            vmem((LS + 16, 128), F32),
            vmem((2, 16, 128), F32),
            vmem((16, LS, 128), F32),
            dma((7,)),
            dma((8,)),
            dma((n_around + 4,)),
            dma((n_around + 4,)),
            dma,
            dma((DEVICES,)),
            dma((n_around + 2,)),
            dma((n_around + 2,)),
            dma,
            dma((16,)),
        ],
        compiler_params=pltpu.CompilerParams(
            collective_id=0, has_side_effects=True, vmem_limit_bytes=60 << 20
        ),
        name="unite",
    )(
        radar_l, radar_s, weights_l, weights_s,
        owner_l.reshape(1, LL), owner_s.reshape(1, LS), slot_l.reshape(1, LL), slot_s.reshape(1, LS), models,
    )


def solution(mesh):
    in_specs = (
        P(None, "sec", "swath"),
        P(None, "sec", "swath"),
        P(("sec", "swath"), None, None),
        P(("sec", "swath"), None, None),
        P(("sec", "swath"), None),
        P(("sec", "swath"), None),
        P(("sec", "swath")),
        P(("sec", "swath")),
        P(),
    )
    out_specs = P(None, "sec", "swath")
    return jax.shard_map(body, mesh=mesh, in_specs=in_specs, out_specs=out_specs, check_vma=False)
```

time: 94.5 us -> 74.5 us (0.79)
  Pallas kernels: 85.9 us -> 70 us
  local copies, waits for them, and re-layouts: 7.98 us -> 4.36 us
    pallas_call x3 -> x1, Pallas kernels: 85.9 us -> 70 us  [body(): pl.pallas_call(main_kernel, out_shape=jax.ShapeDtypeStruct((16, LS, 128),...]
    unnamed x16 -> x1, local copies, waits for them, and re-layouts: 7.3 us -> 3.11 us
where the time goes in v2:
time: 74.5 us; the launch traced here: 74.4 us
  Pallas kernels  70 us (94%)
  local copies, waits for them, and re-layouts  4.36 us (6%)
    pallas_call x1, Pallas kernels, body(): pl.pallas_call(main_kernel, out_shape=jax.ShapeDtypeStruct((16, LS, 128),...  70 us
    unnamed x1, local copies, waits for them, and re-layouts  3.11 us

profile of v2, /device:TPU:1, one launch (start us, length us, event | category | flops | bytes accessed | tf_op | source)
XLA Modules:
  0.0 74.4 jit_solution(4386063438338728899)
XLA Ops:
  0.0 1.2 %reshape.14.slot_l_hbm = s32[1,384]{1,0:T(1,128)} reshape(s32[384]{0:T(512)} %param.15) | data formatting | bytes 3072 | tf_op jit(solution)/shard_map/reshape | solution.py:523
  1.2 70.0 %unite.1 = f32[16,256,128]{2,1,0:T(8,128)} custom-call(bf16[6,384,128]{2,1,0:T(8,128)(2,1)} %radar_l_hbm.1, bf16[6,256,128]{2,1,0:T(8,128)(2,1)} %radar_s_hbm.1, bf16[384,128,128]{2,1,0:T(8,128)(2,1)} %weights_l.1, bf16[256,128,128]{2,1,0:T(8,128)(2,1)} %weights_s.1, s32[1,384]{1,0:T(1,128)} %bitcast.3, s32[1,256]{1,0:T(1,128)} %bitcast.4, ...), custom_call_target="tpu_custom_call" | custom-call | tf_op jit(solution)/shard_map/unite/pallas_call | solution.py:466
  71.2 3.1 %copy.11 = f32[16,256,128]{2,1,0:T(8,128)} copy(f32[16,256,128]{2,1,0:T(8,128)} %unite.1) | data formatting | bytes 4194304

commit v3 on v2

--- a/solution.py
+++ b/solution.py
@@ -18,6 +18,7 @@
 TILES = LL + LS
 ROWS = 64
 MARK_ROW = 30
+FINISH = 4
 TOP_L, TOP_S = 8, 8 + LL + 16
 EXT = LL + LS + 32
 upper_pairs = [(i, j) for i in range(6) for j in range(i, 6)]
@@ -50,7 +51,7 @@
         tile = iota((1, lines), 1) + first
         facts = jnp.concatenate(
             [
-                slot[...].astype(F32),
+                slot[...].reshape(1, lines).astype(F32),
                 lax.rem(tile, 128).astype(F32),
                 lax.div(tile, 128).astype(F32),
                 jnp.ones((1, lines), F32),
@@ -94,6 +95,14 @@
     return jnp.concatenate([big, (x - big.astype(F32)).astype(BF16)], axis=1)
 
 
+def beside_lanes(x, p):
+    lane = iota(x.shape, 1)
+    return (
+        jnp.where(lane == 0, p, pltpu.roll(x, 1, 1)),
+        jnp.where(lane == 127, p, pltpu.roll(x, 127, 1)),
+    )
+
+
 def joint_of(z):
     parts = [z[i] * z[j] + z[6 + i] * z[6 + j] for i, j in upper_pairs]
     parts += [z[6 + i] * z[j] - z[i] * z[6 + j] for i, j in strict_pairs]
@@ -102,15 +111,16 @@
 
 def main_kernel(
     radar_l_hbm, radar_s_hbm, weights_l, weights_s, owner_l_hbm, owner_s_hbm, slot_l_hbm, slot_s_hbm, models_hbm,
-    out_ref,
+    g_ref, turned_ref, halo_lines,
     radar_l, radar_s, owner_l, owner_s, slot_l, slot_s, models,
-    wbuf, xbuf, pbuf, fbuf, vbuf, stage, payload, recv, maskbuf, edge, hcols, hrows,
-    source_v, source, marks, matrix, zmap, zedge, zrows, zcols_in, zrows_in, zv, gbuf, gv, hbuf, halo_lines, obuf,
+    wbuf, xbuf, pbuf, fbuf, stage, payload, recv, maskbuf, edge, hcols, hrows,
+    source_v, source, marks, matrix, zmap, zedge, zrows, zcols_in, zrows_in, zv, gbuf, gv, hbuf,
     in_sem, w_sem, hs_sem, hr_sem, send_sem, recv_sem, es_sem, er_sem, plan_sem, out_sem,
 ):
     sec, swath = lax.axis_index("sec"), lax.axis_index("swath")
     me = sec * N_SWATH + swath
-    my_place = swath * N_SEC + sec
+    turn = lax.rem(swath + sec * 8, N_SWATH)
+    my_place = turn * N_SEC + sec
 
     pairs = (
         (radar_l_hbm, radar_l), (radar_s_hbm, radar_s), (owner_l_hbm, owner_l), (owner_s_hbm, owner_s),
@@ -122,14 +132,22 @@
 
     barrier = pltpu.get_barrier_semaphore()
 
-    def greet(i, _):
-        peer = lax.rem(me + i, DEVICES)
-        pl.semaphore_signal(
-            barrier, inc=1, device_id=(lax.div(peer, N_SWATH), lax.rem(peer, N_SWATH)), device_id_type=MESH
-        )
+    def greet(ds, dw):
+        peer = (lax.rem(sec + ds, N_SEC), lax.rem(swath + dw, N_SWATH))
+        pl.semaphore_signal(barrier, inc=1, device_id=peer, device_id_type=MESH)
+
+    for ds in range(1, N_SEC):
+        greet(ds, 0)
+    for dw in (1, N_SWATH - 1):
+        for ds in range(N_SEC):
+            greet(ds, dw)
+
+    def greet_rest(dw, _):
+        for ds in range(N_SEC):
+            greet(ds, dw)
         return 0
 
-    lax.fori_loop(1, DEVICES, greet, 0)
+    lax.fori_loop(2, N_SWATH - 1, greet_rest, 0)
     for copy in loads:
         copy.wait()
 
@@ -195,7 +213,7 @@
             xbuf[c, top : top + lines, :] = radar[c].astype(F32)
     fbuf[TILES] = jnp.zeros((8, 128), F32)
     fflat = fbuf.reshape((TILES + 1) * 8, 128)
-    vbuf[...] = jnp.zeros((256, 128), F32)
+    stage[...] = jnp.zeros((256, 128), F32)
     zmap[...] = jnp.zeros((2, LS, 768), F32)
     r32 = lax.rem(iota((256, 128), 0), 32)
     for band in range(2):
@@ -238,13 +256,6 @@
         for top, lines, first in ((TOP_L, LL, 0), (TOP_S, LS, 6)):
             xbuf[c, top - 1 : top, :] = hrows[0, first + c].astype(F32)[15:16] * has_up
             xbuf[c, top + lines : top + lines + 1, :] = hrows[1, first + c].astype(F32)[0:1] * has_down
-
-    def beside_lanes(x, p):
-        lane = iota(x.shape, 1)
-        return (
-            jnp.where(lane == 0, p, pltpu.roll(x, 1, 1)),
-            jnp.where(lane == 127, p, pltpu.roll(x, 127, 1)),
-        )
 
     def lines_three(h):
         return (pltpu.roll(h, 1, 0)[8:72], h[8:72], pltpu.roll(h, 79, 0)[8:72])
@@ -274,6 +285,8 @@
             local_mean = (a + b + d) / 9.0
             filtered = local_mean + gain * (x[8:72] - local_mean)
             fflat[pl.ds(tile * 8 + c, 64, stride=8), :] = filtered.astype(BF16).astype(F32)
+        for c in range(6, 8):
+            fflat[pl.ds(tile * 8 + c, 64, stride=8), :] = jnp.zeros((64, 128), F32)
         return 0
 
     lax.fori_loop(0, TILES // 64, filter_chunk, 0)
@@ -282,34 +295,25 @@
     for copy in w_copies:
         copy.wait()
 
-    code_lane = iota((128, 256), 1)
-    r = lax.rem(code_lane, 32)
-    code = jnp.where(r < 3 * CAP, lax.div(lax.rem(code_lane, 128), 64) * 16 + lax.rem(r, CAP), -1)
+    zero = jnp.zeros((16, 128), BF16)
 
     def send_group(i, _):
-        first = lax.rem(swath + i * 13, DEVICES // 4) * 4
-        for j in range(4):
-            for k in range(CAP):
-                v = fbuf[source[k, first + j]]
-                vbuf[pl.ds(j * 64 + k, 3, stride=CAP), :] = v[0:3]
-                vbuf[pl.ds(j * 64 + 32 + k, 3, stride=CAP), :] = v[3:6]
-        v = vbuf[...].astype(BF16)
-        zero = jnp.zeros((128, 128), BF16)
-        rhs = jnp.concatenate(
-            [jnp.concatenate([v[0:128], zero], axis=1), jnp.concatenate([zero, v[128:256]], axis=1)], axis=0
-        )
-        total = jnp.zeros((128, 256), F32)
-        for jj in range(2):
-            both = []
-            for k in range(CAP):
-                wa = wbuf[jnp.minimum(source[k, first + jj], TILES - 1)]
-                wb = wbuf[jnp.minimum(source[k, first + 2 + jj], TILES - 1)]
-                both.append(jnp.concatenate([wa, wb], axis=1))
-            out = dot(jnp.concatenate(both, axis=0), rhs, NT)
-            for k in range(CAP):
-                total = jnp.where(code == jj * 16 + k, out[k * 128 : (k + 1) * 128], total)
-        stage[0:128] = total[:, 0:128].T
-        stage[128:256] = total[:, 128:256].T
+        first = lax.rem(turn + i * 13, DEVICES // 4) * 4
+        for k in range(CAP):
+            v = [fbuf[source[k, first + j]] for j in range(4)]
+            w = [wbuf[jnp.minimum(source[k, first + j], TILES - 1)] for j in range(4)]
+            top = jnp.concatenate([v[0], v[2]], axis=0).astype(BF16)
+            bottom = jnp.concatenate([v[1], v[3]], axis=0).astype(BF16)
+            lhs = jnp.concatenate(
+                [jnp.concatenate([top, zero], axis=1), jnp.concatenate([zero, bottom], axis=1)], axis=0
+            )
+            rhs = jnp.concatenate(
+                [jnp.concatenate([w[0], w[1]], axis=1), jnp.concatenate([w[2], w[3]], axis=1)], axis=0
+            )
+            out = dot(lhs, rhs, NT)
+            for j, part in enumerate((out[0:8, 0:128], out[16:24, 0:128], out[8:16, 128:256], out[24:32, 128:256])):
+                stage[pl.ds(j * 64 + k, 3, stride=CAP), :] = part[0:3]
+                stage[pl.ds(j * 64 + 32 + k, 3, stride=CAP), :] = part[3:6]
         for j in range(4):
             o = first + j
             stage[j * 64 + MARK_ROW : j * 64 + MARK_ROW + 1, :] = marks[pl.ds(o, 1), :]
@@ -397,6 +401,21 @@
         return 0
 
     lax.fori_loop(0, LS // 16, fit_lines, 0)
+    hbuf[0:8] = jnp.zeros((8, 128), F32)
+    hbuf[8 + LS : 16 + LS] = jnp.zeros((8, 128), F32)
+    no_lane = jnp.zeros((LS, 128), F32)
+
+    def window(k, _):
+        cells = gbuf[k]
+        left, right = beside_lanes(cells, no_lane)
+        three = cells + left + right
+        hbuf[8 : 8 + LS] = three
+        gbuf[k] = hbuf[7 : 7 + LS] + three + hbuf[9 : 9 + LS]
+        return 0
+
+    lax.fori_loop(0, 16, window, 0)
+    g_copy = pltpu.make_async_copy(gbuf, g_ref, out_sem)
+    g_copy.start()
 
     for copy in last:
         copy.wait()
@@ -434,53 +453,70 @@
             + jnp.where(lane16 == 127, right, pltpu.roll(edge_line, 127, 1))
         )
     turned = g.T
-    turned = halves(jnp.concatenate([turned, pltpu.roll(turned, 127, 1)], axis=0))
-
-    def finish(k, _):
-        place = jnp.where(
-            ((qr == k * 8) & (qc == 0)) | ((qr == k * 8 + 2) & (qc == 127)), 1.0, 0.0
-        ).astype(BF16)
-        beside_block = dot(turned, place)
-        own_cells = gbuf[k]
-        left, right = beside_lanes(own_cells, beside_block)
-        hbuf[8 : 8 + LS] = own_cells + left + right
-        hbuf[7:8] = halo_lines[0, pl.ds(k, 1), :]
-        hbuf[8 + LS : 9 + LS] = halo_lines[1, pl.ds(k, 1), :]
-        obuf[k] = hbuf[7 : 7 + LS] + hbuf[8 : 8 + LS] + hbuf[9 : 9 + LS]
-        pltpu.make_async_copy(obuf.at[k], out_ref.at[k], out_sem.at[k]).start()
-        return 0
-
-    lax.fori_loop(0, 16, finish, 0)
+    columns = jnp.concatenate([turned, pltpu.roll(turned, 127, 1)], axis=0)
+    hbuf[7:8] = jnp.zeros((1, 128), F32)
+    hbuf[8 : 8 + LS] = columns
+    hbuf[8 + LS : 9 + LS] = jnp.zeros((1, 128), F32)
+    turned_ref[...] = halves(hbuf[7 : 7 + LS] + columns + hbuf[9 : 9 + LS])
     pltpu.make_async_copy(payload.at[pl.ds(0, DEVICES - 1)], payload.at[pl.ds(0, DEVICES - 1)], send_sem).wait()
-
-    def written(k, _):
-        pltpu.make_async_copy(obuf.at[k], out_ref.at[k], out_sem.at[k]).wait()
-        return 0
-
-    lax.fori_loop(0, 16, written, 0)
+    g_copy.wait()
+
+
+def finish_kernel(cells_hbm, columns_hbm, lines_hbm, out_hbm, cells, columns, halo_lines, in_sem, small_sem, out_sem):
+    small = [
+        pltpu.make_async_copy(columns_hbm, columns, small_sem.at[0]),
+        pltpu.make_async_copy(lines_hbm, halo_lines, small_sem.at[1]),
+    ]
+    parts = 16 // FINISH
+
+    def moved(src, dst, sem):
+        return [
+            pltpu.make_async_copy(src.at[pl.ds(n * FINISH, FINISH)], dst.at[pl.ds(n * FINISH, FINISH)], sem.at[n])
+            for n in range(parts)
+        ]
+
+    loads, stores = moved(cells_hbm, cells, in_sem), moved(cells, out_hbm, out_sem)
+    for copy in small + loads:
+        copy.start()
+    for copy in small:
+        copy.wait()
+    qr, qc = lax.rem(iota((256, 128), 0), 128), iota((256, 128), 1)
+    for n in range(parts):
+        loads[n].wait()
+        for k in range(n * FINISH, (n + 1) * FINISH):
+            place = jnp.where(((qr == k * 8) & (qc == 0)) | ((qr == k * 8 + 2) & (qc == 127)), 1.0, 0.0).astype(BF16)
+            cells[k] = cells[k] + dot(columns[...], place)
+            cells[k, 0:1] = cells[k, 0:1] + halo_lines[0, k : k + 1]
+            cells[k, LS - 1 : LS] = cells[k, LS - 1 : LS] + halo_lines[1, k : k + 1]
+        stores[n].start()
+    for copy in stores:
+        copy.wait()
 
 
 def body(radar_l, radar_s, weights_l, weights_s, owner_l, owner_s, slot_l, slot_s, models):
     dma, n_around = pltpu.SemaphoreType.DMA, len(AROUND)
     vmem = pltpu.VMEM
-    return pl.pallas_call(
+    cells, turned, halo_lines = pl.pallas_call(
         main_kernel,
-        out_shape=jax.ShapeDtypeStruct((16, LS, 128), F32),
+        out_shape=(
+            jax.ShapeDtypeStruct((16, LS, 128), F32),
+            jax.ShapeDtypeStruct((256, 256), BF16),
+            jax.ShapeDtypeStruct((2, 16, 128), F32),
+        ),
         in_specs=[pl.BlockSpec(memory_space=pl.ANY)] * 9,
-        out_specs=pl.BlockSpec(memory_space=pl.ANY),
+        out_specs=[pl.BlockSpec(memory_space=pl.ANY)] + [pl.BlockSpec(memory_space=pltpu.VMEM)] * 2,
         scratch_shapes=[
             vmem((6, LL, 128), BF16),
             vmem((6, LS, 128), BF16),
             vmem((1, LL), I32),
             vmem((1, LS), I32),
-            vmem((1, LL), I32),
-            vmem((1, LS), I32),
+            vmem((LL,), I32),
+            vmem((LS,), I32),
             vmem((16, NJ), F32),
             vmem((TILES, 128, 128), BF16),
             vmem((6, EXT, 128), F32),
             vmem((6, EXT, 128), F32),
             vmem((TILES + 1, 8, 128), F32),
-            vmem((256, 128), F32),
             vmem((256, 128), F32),
             vmem((DEVICES, ROWS, 128), BF16),
             vmem((DEVICES, ROWS, 128), BF16),
@@ -501,8 +537,6 @@
             vmem((16, LS, 128), F32),
             vmem((128, 128), F32),
             vmem((LS + 16, 128), F32),
-            vmem((2, 16, 128), F32),
-            vmem((16, LS, 128), F32),
             dma((7,)),
             dma((8,)),
             dma((n_around + 4,)),
@@ -512,7 +546,7 @@
             dma((n_around + 2,)),
             dma((n_around + 2,)),
             dma,
-            dma((16,)),
+            dma,
         ],
         compiler_params=pltpu.CompilerParams(
             collective_id=0, has_side_effects=True, vmem_limit_bytes=60 << 20
@@ -520,8 +554,24 @@
         name="unite",
     )(
         radar_l, radar_s, weights_l, weights_s,
-        owner_l.reshape(1, LL), owner_s.reshape(1, LS), slot_l.reshape(1, LL), slot_s.reshape(1, LS), models,
+        owner_l.reshape(1, LL), owner_s.reshape(1, LS), slot_l, slot_s, models,
     )
+    return pl.pallas_call(
+        finish_kernel,
+        out_shape=jax.ShapeDtypeStruct((16, LS, 128), F32),
+        in_specs=[pl.BlockSpec(memory_space=pl.ANY)] * 3,
+        out_specs=pl.BlockSpec(memory_space=pl.ANY),
+        scratch_shapes=[
+            vmem((16, LS, 128), F32),
+            vmem((256, 256), BF16),
+            vmem((2, 16, 128), F32),
+            dma((16 // FINISH,)),
+            dma((2,)),
+            dma((16 // FINISH,)),
+        ],
+        compiler_params=pltpu.CompilerParams(vmem_limit_bytes=60 << 20),
+        name="finish",
+    )(cells, turned, halo_lines)
 
 
 def solution(mesh):

time: 74.5 us -> 64.2 us (0.86)
  Pallas kernels: 70 us -> 64.1 us
  local copies, waits for them, and re-layouts: 4.36 us -> 0 us
    pallas_call x1 -> x2, Pallas kernels: 70 us -> 64.1 us  [the longest x1 60.7 us: body(): pl.pallas_call(main_kernel, out_shape=(jax.ShapeDtypeStruct((16, LS, 128)...]
    unnamed x1 -> x0, local copies, waits for them, and re-layouts: 3.11 us -> none
    reshape x1 -> x0, local copies, waits for them, and re-layouts: 1.24 us -> none  [body(): slot_l.reshape(1, LL)]
where the time goes in v3:
time: 64.2 us; the launch traced here: 64.1 us
  Pallas kernels  64.1 us (100%)
    pallas_call x1, Pallas kernels, body(): pl.pallas_call(main_kernel, out_shape=(jax.ShapeDtypeStruct((16, LS, 128)...  60.7 us
    pallas_call x1, Pallas kernels, body(): pl.pallas_call(finish_kernel, out_shape=jax.ShapeDtypeStruct((16, LS, 128...  3.33 us

profile of v3, /device:TPU:1, one launch (start us, length us, event | category | flops | bytes accessed | tf_op | source)
XLA Modules:
  0.0 64.1 jit_solution(1371010893576423938)
XLA Ops:
  0.0 60.7 %unite.1 = (f32[16,256,128]{2,1,0:T(8,128)}, bf16[256,256]{1,0:T(8,128)(2,1)}, f32[2,16,128]{2,1,0:T(8,128)}) custom-call(bf16[6,384,128]{2,1,0:T(8,128)(2,1)} %radar_l_hbm.1, bf16[6,256,128]{2,1,0:T(8,128)(2,1)} %radar_s_hbm.1, bf16[384,128,128]{2,1,0:T(8,128)(2,1)} %weights_l.1, bf16[256,128,128]{2,1,0:T(8,128)(2,1)} %weights_s.1, s32[1,384]{1,0:T(1,128)} %bitcast.2, ...), custom_call_target="tpu_custom_call" | custom-call | tf_op jit(solution)/shard_map/unite/pallas_call | solution.py:499
  60.7 3.3 %finish.1 = f32[16,256,128]{2,1,0:T(8,128)} custom-call(f32[16,256,128]{2,1,0:T(8,128)} %get-tuple-element.8.cells_hbm, bf16[256,256]{1,0:T(8,128)(2,1)} %get-tuple-element.9.columns_hbm, f32[2,16,128]{2,1,0:T(8,128)} %get-tuple-element.10.lines_hbm), custom_call_target="tpu_custom_call" | custom-call | tf_op jit(solution)/shard_map/finish/pallas_call | solution.py:559

commit v4 on v3

--- a/solution.py
+++ b/solution.py
@@ -24,7 +24,6 @@
 upper_pairs = [(i, j) for i in range(6) for j in range(i, 6)]
 strict_pairs = [(i, j) for i in range(6) for j in range(i + 1, 6)]
 NJ = len(upper_pairs) + len(strict_pairs)
-AROUND = [(0, -1), (0, 1), (-1, -1), (-1, 1), (1, -1), (1, 1)]
 
 
 def iota(shape, dim):
@@ -113,8 +112,8 @@
     radar_l_hbm, radar_s_hbm, weights_l, weights_s, owner_l_hbm, owner_s_hbm, slot_l_hbm, slot_s_hbm, models_hbm,
     g_ref, turned_ref, halo_lines,
     radar_l, radar_s, owner_l, owner_s, slot_l, slot_s, models,
-    wbuf, xbuf, pbuf, fbuf, stage, payload, recv, maskbuf, edge, hcols, hrows,
-    source_v, source, marks, matrix, zmap, zedge, zrows, zcols_in, zrows_in, zv, gbuf, gv, hbuf,
+    wbuf, xbuf, pbuf, fbuf, stage, payload, recv, maskbuf, edge, edge_rows, hcols, hcorners, hrows,
+    source_v, source, marks, matrix, zmap, zedge, zrows, zcols_in, zcorners, zrows_in, zv, gbuf, gv, hbuf,
     in_sem, w_sem, hs_sem, hr_sem, send_sem, recv_sem, es_sem, er_sem, plan_sem, out_sem,
 ):
     sec, swath = lax.axis_index("sec"), lax.axis_index("swath")
@@ -152,6 +151,7 @@
         copy.wait()
 
     column, row = iota((16, 128), 1), iota((16, 128), 0)
+    ends = jnp.zeros((16, 128), F32)
     for radar, first, lines in ((radar_l, 0, LL), (radar_s, LL, LS)):
         total = jnp.zeros((16, lines), F32)
         for c in range(6):
@@ -160,34 +160,37 @@
             ).astype(BF16)
             total = total + dot(pick, radar[c], NT)
         edge[:, first : first + lines] = total.astype(BF16)
+        at = 0 if first == 0 else 2
+        ends = jnp.where(column == at, total[:, 0:1], ends)
+        ends = jnp.where(column == at + 1, total[:, lines - 1 : lines], ends)
+    edge[:, TILES : TILES + 128] = ends.astype(BF16)
+    for end in range(2):
+        lines_at_end = [
+            radar[c, lines - 16 : lines, :].astype(F32)[15:16] if end else radar[c, 0:16, :].astype(F32)[0:1]
+            for radar, lines in ((radar_l, LL), (radar_s, LS))
+            for c in range(6)
+        ]
+        edge_rows[end] = jnp.concatenate(lines_at_end + [jnp.zeros((4, 128), F32)], axis=0).astype(BF16)
 
     pl.semaphore_wait(barrier, DEVICES - 1)
 
     def beside(ds, dw):
         return (lax.rem(sec + ds + N_SEC, N_SEC), lax.rem(swath + dw + N_SWATH, N_SWATH))
 
-    def around(src, slots, ssem, rsem):
+    def sends(moves, ssem, rsem):
         return [
             pltpu.make_async_remote_copy(
-                src_ref=src, dst_ref=slots.at[n], send_sem=ssem.at[n], recv_sem=rsem.at[n],
-                device_id=beside(-ds, -dw), device_id_type=MESH,
+                src_ref=src, dst_ref=dst, send_sem=ssem.at[n], recv_sem=rsem.at[n],
+                device_id=beside(ds, dw), device_id_type=MESH,
             )
-            for n, (ds, dw) in enumerate(AROUND)
+            for n, (src, dst, ds, dw) in enumerate(moves)
         ]
 
-    halo = around(edge, hcols, hs_sem, hr_sem)
-    n = len(AROUND)
-    for radar, first, lines in ((radar_l, 0, LL), (radar_s, 6, LS)):
-        for side, (start, ds) in enumerate(((lines - 16, 1), (0, -1))):
-            halo.append(
-                pltpu.make_async_remote_copy(
-                    src_ref=radar.at[:, pl.ds(start, 16), :],
-                    dst_ref=hrows.at[side, pl.ds(first, 6)],
-                    send_sem=hs_sem.at[n], recv_sem=hr_sem.at[n],
-                    device_id=beside(ds, 0), device_id_type=MESH,
-                )
-            )
-            n += 1
+    moves = [(edge.at[:, pl.ds(0, TILES)], hcols.at[0], 0, -1), (edge.at[:, pl.ds(0, TILES)], hcols.at[1], 0, 1)]
+    for n, (ds, dw) in enumerate(((1, -1), (1, 1), (-1, -1), (-1, 1))):
+        moves.append((edge.at[:, pl.ds(TILES, 128)], hcorners.at[n], ds, dw))
+    moves += [(edge_rows.at[1], hrows.at[0], 1, 0), (edge_rows.at[0], hrows.at[1], -1, 0)]
+    halo = sends(moves, hs_sem, hr_sem)
     for copy in halo:
         copy.start()
 
@@ -228,22 +231,22 @@
 
     has_up, has_down = flag(sec > 0), flag(sec < N_SEC - 1)
     has_left, has_right = flag(swath > 0), flag(swath < N_SWATH - 1)
-    low = iota((16, TILES), 0) < 8
-    side = jnp.where(low, has_right, has_left)
-
-    def pick_sides(left_n, right_n):
-        return jnp.where(low, hcols[right_n].astype(F32), hcols[left_n].astype(F32)) * side
-
-    middle = pick_sides(0, 1)
-    up, down = pick_sides(2, 3) * has_up, pick_sides(4, 5) * has_down
-    corner_lane = iota((16, 128), 1)
-    corners = jnp.where(corner_lane == 0, up[:, LL - 1 : LL], 0.0)
-    corners = jnp.where(corner_lane == 1, down[:, 0:1], corners)
-    corners = jnp.where(corner_lane == 2, up[:, TILES - 1 : TILES], corners)
-    corners = jnp.where(corner_lane == 3, down[:, LL : LL + 1], corners)
+
+    def merge(right, left):
+        low = iota(right.shape, 0) < 8
+        return jnp.where(low, right.astype(F32) * has_right, left.astype(F32) * has_left)
+
+    middle = merge(hcols[0], hcols[1])
+    up = merge(hcorners[0], hcorners[1]) * has_up
+    down = merge(hcorners[2], hcorners[3]) * has_down
+    corners = jnp.where(column == 0, up[:, 1:2], 0.0)
+    corners = jnp.where(column == 1, down[:, 0:1], corners)
+    corners = jnp.where(column == 2, up[:, 3:4], corners)
+    corners = jnp.where(column == 3, down[:, 2:3], corners)
     lines_of = jnp.concatenate([middle, corners], axis=1)
     lines_of = jnp.concatenate([lines_of, jnp.zeros((112, TILES + 128), F32)], axis=0).T.astype(BF16)
     pr, pc = iota((128, 128), 0), iota((128, 128), 1)
+    above, below = hrows[0].astype(F32) * has_up, hrows[1].astype(F32) * has_down
     for c in range(6):
         place = jnp.where(((pr == 8 + c) & (pc == 0)) | ((pr == c) & (pc == 127)), 1.0, 0.0).astype(BF16)
         placed = dot(lines_of, place)
@@ -254,8 +257,8 @@
         pbuf[c, TOP_S - 1 : TOP_S, :] = placed[TILES + 2 : TILES + 3]
         pbuf[c, TOP_S + LS : TOP_S + LS + 1, :] = placed[TILES + 3 : TILES + 4]
         for top, lines, first in ((TOP_L, LL, 0), (TOP_S, LS, 6)):
-            xbuf[c, top - 1 : top, :] = hrows[0, first + c].astype(F32)[15:16] * has_up
-            xbuf[c, top + lines : top + lines + 1, :] = hrows[1, first + c].astype(F32)[0:1] * has_down
+            xbuf[c, top - 1 : top, :] = above[first + c : first + c + 1]
+            xbuf[c, top + lines : top + lines + 1, :] = below[first + c : first + c + 1]
 
     def lines_three(h):
         return (pltpu.roll(h, 1, 0)[8:72], h[8:72], pltpu.roll(h, 79, 0)[8:72])
@@ -373,17 +376,22 @@
         zrows[16 + n : 17 + n, :] = z[LS - 1 : LS]
     zrows[12:16, :] = jnp.zeros((4, 128), F32)
     zrows[28:32, :] = jnp.zeros((4, 128), F32)
-    zedge[...] = packed.T[0:32]
-    last = around(zedge, zcols_in, es_sem, er_sem)
-    n = len(AROUND)
-    for side_n, ds in enumerate((1, -1)):
-        last.append(
-            pltpu.make_async_remote_copy(
-                src_ref=zrows, dst_ref=zrows_in.at[side_n], send_sem=es_sem.at[n], recv_sem=er_sem.at[n],
-                device_id=beside(ds, 0), device_id_type=MESH,
-            )
-        )
-        n += 1
+    turned_edges = packed.T[0:32]
+    zedge[:, 0:LS] = turned_edges
+    corner_lane = iota((32, 128), 1)
+    zedge[:, LS : LS + 128] = jnp.where(corner_lane == 0, turned_edges[:, 0:1], turned_edges[:, LS - 1 : LS])
+    moves = [
+        (zedge.at[pl.ds(0, 16), pl.ds(0, LS)], zcols_in.at[pl.ds(0, 16)], 0, -1),
+        (zedge.at[pl.ds(16, 16), pl.ds(0, LS)], zcols_in.at[pl.ds(16, 16)], 0, 1),
+    ]
+    for n, (ds, dw) in enumerate(((1, -1), (1, 1), (-1, -1), (-1, 1))):
+        part = pl.ds((n % 2) * 16, 16)
+        moves.append((zedge.at[part, pl.ds(LS, 128)], zcorners.at[n // 2, part], ds, dw))
+    moves += [
+        (zrows.at[pl.ds(16, 16)], zrows_in.at[0], 1, 0),
+        (zrows.at[pl.ds(0, 16)], zrows_in.at[1], -1, 0),
+    ]
+    last = sends(moves, es_sem, er_sem)
     for copy in last:
         copy.start()
 
@@ -413,30 +421,28 @@
         gbuf[k] = hbuf[7 : 7 + LS] + three + hbuf[9 : 9 + LS]
         return 0
 
-    lax.fori_loop(0, 16, window, 0)
-    g_copy = pltpu.make_async_copy(gbuf, g_ref, out_sem)
-    g_copy.start()
+    g_copies = []
+    for n in range(4):
+        lax.fori_loop(n * 4, n * 4 + 4, window, 0)
+        g_copies.append(
+            pltpu.make_async_copy(gbuf.at[pl.ds(n * 4, 4)], g_ref.at[pl.ds(n * 4, 4)], out_sem.at[n])
+        )
+        g_copies[-1].start()
 
     for copy in last:
         copy.wait()
 
-    low = iota((32, LS), 0) < 16
-    side = jnp.where(low, has_right, has_left)
-
-    def pick_map_sides(left_n, right_n):
-        return jnp.where(low, zcols_in[right_n], zcols_in[left_n]) * side
-
-    middle = pick_map_sides(0, 1)
-    up, down = pick_map_sides(2, 3) * has_up, pick_map_sides(4, 5) * has_down
-    corner_lane = iota((32, 128), 1)
-    corners = jnp.where(lax.rem(corner_lane, 2) == 0, up[:, LS - 1 : LS], down[:, 0:1])
+    side = jnp.where(iota((32, 1), 0) < 16, has_right, has_left)
+    middle = zcols_in[...] * side
+    up, down = zcorners[0] * (side * has_up), zcorners[1] * (side * has_down)
+    corners = jnp.where(lax.rem(corner_lane, 2) == 0, up[:, 1:2], down[:, 0:1])
     for n in range(12):
         zv[n, 0:1] = middle[16 + n : 17 + n, 0:128]
         zv[n, 1:2] = middle[16 + n : 17 + n, 128:256]
         zv[n, 2:3] = middle[n : n + 1, 0:128]
         zv[n, 3:4] = middle[n : n + 1, 128:256]
         zv[n, 4:5] = jnp.where(mark_lane < 2, corners[16 + n : 17 + n], corners[n : n + 1])
-        zv[n, 5:6] = zrows_in[0, 16 + n : 17 + n] * has_up
+        zv[n, 5:6] = zrows_in[0, n : n + 1] * has_up
         zv[n, 6:7] = zrows_in[1, n : n + 1] * has_down
         zv[n, 7:8] = jnp.zeros((1, 128), F32)
     g = dot(matrix[...], joint_of([zv[n] for n in range(12)]).astype(BF16))
@@ -459,7 +465,8 @@
     hbuf[8 + LS : 9 + LS] = jnp.zeros((1, 128), F32)
     turned_ref[...] = halves(hbuf[7 : 7 + LS] + columns + hbuf[9 : 9 + LS])
     pltpu.make_async_copy(payload.at[pl.ds(0, DEVICES - 1)], payload.at[pl.ds(0, DEVICES - 1)], send_sem).wait()
-    g_copy.wait()
+    for copy in g_copies:
+        copy.wait()
 
 
 def finish_kernel(cells_hbm, columns_hbm, lines_hbm, out_hbm, cells, columns, halo_lines, in_sem, small_sem, out_sem):
@@ -494,7 +501,7 @@
 
 
 def body(radar_l, radar_s, weights_l, weights_s, owner_l, owner_s, slot_l, slot_s, models):
-    dma, n_around = pltpu.SemaphoreType.DMA, len(AROUND)
+    dma = pltpu.SemaphoreType.DMA
     vmem = pltpu.VMEM
     cells, turned, halo_lines = pl.pallas_call(
         main_kernel,
@@ -521,32 +528,35 @@
             vmem((DEVICES, ROWS, 128), BF16),
             vmem((DEVICES, ROWS, 128), BF16),
             vmem((6, 256, 128), BF16),
-            vmem((16, TILES), BF16),
-            vmem((n_around, 16, TILES), BF16),
-            vmem((2, 12, 16, 128), BF16),
+            vmem((16, TILES + 128), BF16),
+            vmem((2, 16, 128), BF16),
+            vmem((2, 16, TILES), BF16),
+            vmem((4, 16, 128), BF16),
+            vmem((2, 16, 128), BF16),
             vmem((16, DEVICES), I32),
             pltpu.SMEM((16, DEVICES), I32),
             vmem((DEVICES, 128), F32),
             vmem((256, NJ * 8), BF16),
             vmem((2, LS, 768), F32),
+            vmem((32, LS + 128), F32),
+            vmem((32, 128), F32),
             vmem((32, LS), F32),
-            vmem((32, 128), F32),
-            vmem((n_around, 32, LS), F32),
             vmem((2, 32, 128), F32),
+            vmem((2, 16, 128), F32),
             vmem((12, 8, 128), F32),
             vmem((16, LS, 128), F32),
             vmem((128, 128), F32),
             vmem((LS + 16, 128), F32),
             dma((7,)),
             dma((8,)),
-            dma((n_around + 4,)),
-            dma((n_around + 4,)),
+            dma((8,)),
+            dma((8,)),
             dma,
             dma((DEVICES,)),
-            dma((n_around + 2,)),
-            dma((n_around + 2,)),
+            dma((8,)),
+            dma((8,)),
             dma,
-            dma,
+            dma((4,)),
         ],
         compiler_params=pltpu.CompilerParams(
             collective_id=0, has_side_effects=True, vmem_limit_bytes=60 << 20

time: 64.2 us -> 61.4 us (0.956)
  Pallas kernels: 64.1 us -> 61.3 us
    pallas_call x1, Pallas kernels: 60.7 us -> 57.9 us  [body(): pl.pallas_call(main_kernel, out_shape=(jax.ShapeDtypeStruct((16, LS, 128)...]
where the time goes in v4:
time: 61.4 us; the launch traced here: 61.3 us
  Pallas kernels  61.3 us (100%)
    pallas_call x1, Pallas kernels, body(): pl.pallas_call(main_kernel, out_shape=(jax.ShapeDtypeStruct((16, LS, 128)...  57.9 us
    pallas_call x1, Pallas kernels, body(): pl.pallas_call(finish_kernel, out_shape=jax.ShapeDtypeStruct((16, LS, 128...  3.33 us

profile of v4, /device:TPU:1, one launch (start us, length us, event | category | flops | bytes accessed | tf_op | source)
XLA Modules:
  0.0 61.3 jit_solution(2063406328824109533)
XLA Ops:
  0.0 57.9 %unite.1 = (f32[16,256,128]{2,1,0:T(8,128)}, bf16[256,256]{1,0:T(8,128)(2,1)}, f32[2,16,128]{2,1,0:T(8,128)}) custom-call(bf16[6,384,128]{2,1,0:T(8,128)(2,1)} %radar_l_hbm.1, bf16[6,256,128]{2,1,0:T(8,128)(2,1)} %radar_s_hbm.1, bf16[384,128,128]{2,1,0:T(8,128)(2,1)} %weights_l.1, bf16[256,128,128]{2,1,0:T(8,128)(2,1)} %weights_s.1, s32[1,384]{1,0:T(1,128)} %bitcast.2, ...), custom_call_target="tpu_custom_call" | custom-call | tf_op jit(solution)/shard_map/unite/pallas_call | solution.py:506
  57.9 3.3 %finish.1 = f32[16,256,128]{2,1,0:T(8,128)} custom-call(f32[16,256,128]{2,1,0:T(8,128)} %get-tuple-element.8.cells_hbm, bf16[256,256]{1,0:T(8,128)(2,1)} %get-tuple-element.9.columns_hbm, f32[2,16,128]{2,1,0:T(8,128)} %get-tuple-element.10.lines_hbm), custom_call_target="tpu_custom_call" | custom-call | tf_op jit(solution)/shard_map/finish/pallas_call | solution.py:569

commit v5 on v4

--- a/solution.py
+++ b/solution.py
@@ -396,34 +396,35 @@
         copy.start()
 
     def fit_lines(b, _):
-        at = pl.multiple_of(b * 16, 16)
-        both = []
-        for part in range(2):
-            z = [zmap[n // 6, pl.ds(at + part * 8, 8), (n % 6) * 128 : (n % 6 + 1) * 128] for n in range(12)]
-            both.append(joint_of(z))
-        g = dot(matrix[...], jnp.concatenate(both, axis=1).astype(BF16))
-        g = g[0:128] + g[128:256]
-        for k in range(16):
-            gbuf[k, pl.ds(at, 8), :] = g[k * 8 : k * 8 + 8, 0:128]
-            gbuf[k, pl.ds(at + 8, 8), :] = g[k * 8 : k * 8 + 8, 128:256]
+        for step in range(2):
+            at = pl.multiple_of(b * 32 + step * 16, 16)
+            both = []
+            for part in range(2):
+                z = [zmap[n // 6, pl.ds(at + part * 8, 8), (n % 6) * 128 : (n % 6 + 1) * 128] for n in range(12)]
+                both.append(joint_of(z))
+            g = dot(matrix[...], jnp.concatenate(both, axis=1).astype(BF16))
+            g = g[0:128] + g[128:256]
+            for k in range(16):
+                gbuf[k, pl.ds(at, 8), :] = g[k * 8 : k * 8 + 8, 0:128]
+                gbuf[k, pl.ds(at + 8, 8), :] = g[k * 8 : k * 8 + 8, 128:256]
         return 0
 
-    lax.fori_loop(0, LS // 16, fit_lines, 0)
-    hbuf[0:8] = jnp.zeros((8, 128), F32)
-    hbuf[8 + LS : 16 + LS] = jnp.zeros((8, 128), F32)
+    lax.fori_loop(0, LS // 32, fit_lines, 0)
+    hbuf[:, 0:8] = jnp.zeros((4, 8, 128), F32)
+    hbuf[:, 8 + LS : 16 + LS] = jnp.zeros((4, 8, 128), F32)
     no_lane = jnp.zeros((LS, 128), F32)
 
-    def window(k, _):
+    def window(k, slot):
         cells = gbuf[k]
         left, right = beside_lanes(cells, no_lane)
         three = cells + left + right
-        hbuf[8 : 8 + LS] = three
-        gbuf[k] = hbuf[7 : 7 + LS] + three + hbuf[9 : 9 + LS]
-        return 0
+        hbuf[slot, 8 : 8 + LS] = three
+        gbuf[k] = hbuf[slot, 7 : 7 + LS] + three + hbuf[slot, 9 : 9 + LS]
 
     g_copies = []
     for n in range(4):
-        lax.fori_loop(n * 4, n * 4 + 4, window, 0)
+        for slot in range(4):
+            window(n * 4 + slot, slot)
         g_copies.append(
             pltpu.make_async_copy(gbuf.at[pl.ds(n * 4, 4)], g_ref.at[pl.ds(n * 4, 4)], out_sem.at[n])
         )
@@ -460,10 +461,8 @@
         )
     turned = g.T
     columns = jnp.concatenate([turned, pltpu.roll(turned, 127, 1)], axis=0)
-    hbuf[7:8] = jnp.zeros((1, 128), F32)
-    hbuf[8 : 8 + LS] = columns
-    hbuf[8 + LS : 9 + LS] = jnp.zeros((1, 128), F32)
-    turned_ref[...] = halves(hbuf[7 : 7 + LS] + columns + hbuf[9 : 9 + LS])
+    hbuf[0, 8 : 8 + LS] = columns
+    turned_ref[...] = halves(hbuf[0, 7 : 7 + LS] + columns + hbuf[0, 9 : 9 + LS])
     pltpu.make_async_copy(payload.at[pl.ds(0, DEVICES - 1)], payload.at[pl.ds(0, DEVICES - 1)], send_sem).wait()
     for copy in g_copies:
         copy.wait()
@@ -546,7 +545,7 @@
             vmem((12, 8, 128), F32),
             vmem((16, LS, 128), F32),
             vmem((128, 128), F32),
-            vmem((LS + 16, 128), F32),
+            vmem((4, LS + 16, 128), F32),
             dma((7,)),
             dma((8,)),
             dma((8,)),

time: 61.4 us -> 59.9 us (0.976)
  Pallas kernels: 61.3 us -> 59.7 us
    pallas_call x1, Pallas kernels: 57.9 us -> 56.4 us  [body(): pl.pallas_call(main_kernel, out_shape=(jax.ShapeDtypeStruct((16, LS, 128)...]
where the time goes in v5:
time: 59.9 us; the launch traced here: 59.7 us
  Pallas kernels  59.7 us (100%)
    pallas_call x1, Pallas kernels, body(): pl.pallas_call(main_kernel, out_shape=(jax.ShapeDtypeStruct((16, LS, 128)...  56.4 us
    pallas_call x1, Pallas kernels, body(): pl.pallas_call(finish_kernel, out_shape=jax.ShapeDtypeStruct((16, LS, 128...  3.33 us

profile of v5, /device:TPU:1, one launch (start us, length us, event | category | flops | bytes accessed | tf_op | source)
XLA Modules:
  0.0 59.7 jit_solution(2452609987418628726)
XLA Ops:
  0.0 56.4 %unite.1 = (f32[16,256,128]{2,1,0:T(8,128)}, bf16[256,256]{1,0:T(8,128)(2,1)}, f32[2,16,128]{2,1,0:T(8,128)}) custom-call(bf16[6,384,128]{2,1,0:T(8,128)(2,1)} %radar_l_hbm.1, bf16[6,256,128]{2,1,0:T(8,128)(2,1)} %radar_s_hbm.1, bf16[384,128,128]{2,1,0:T(8,128)(2,1)} %weights_l.1, bf16[256,128,128]{2,1,0:T(8,128)(2,1)} %weights_s.1, s32[1,384]{1,0:T(1,128)} %bitcast.2, ...), custom_call_target="tpu_custom_call" | custom-call | tf_op jit(solution)/shard_map/unite/pallas_call | solution.py:505
  56.4 3.3 %finish.1 = f32[16,256,128]{2,1,0:T(8,128)} custom-call(f32[16,256,128]{2,1,0:T(8,128)} %get-tuple-element.8.cells_hbm, bf16[256,256]{1,0:T(8,128)(2,1)} %get-tuple-element.9.columns_hbm, f32[2,16,128]{2,1,0:T(8,128)} %get-tuple-element.10.lines_hbm), custom_call_target="tpu_custom_call" | custom-call | tf_op jit(solution)/shard_map/finish/pallas_call | solution.py:568
